TPU v7x, 32 devices: a whole 2x2x4 slice. The times are simulated.
32 devices in a mesh: blk: 16 (over z, x, core), uly: 2 (over y).
Axes of the slice: x: 2, y: 2, z: 4, core: 2. Of those that a mesh axis runs over, the one named last changes fastest.
Arguments:
- queries: bfloat16 [16384, 2048], P(('blk', 'uly'))
- keys: bfloat16 [16384, 256], P(('blk', 'uly'))
- values: bfloat16 [16384, 256], P(('blk', 'uly')), may hold values from -6 to 6
- chosen: int32 [32, 2, 2], replicated, may hold values from 0 to 30, as said below
Outputs:
- attended: bfloat16 [16384, 2048], P(('blk', 'uly'))
Inputs may be any that keep to these rules, and one draw needn't show every extreme that they name: For attention block j and key-value head h, chosen[j, h, 0] and chosen[j, h, 1] differ; for j >= 2 both are below j; for j < 2 at least one is not below j. An id that is not below j selects nothing.
All inputs are finite; a program needn't handle non-finite values.
Results may differ from a plain program's by a relative error of at most 0.0046.
Values may be sent and summed in bfloat16 or wider, within the bound.
No kernel may reach another device: no remote copies, remote signals or barrier semaphores. Data moves between devices by JAX's collectives and lax.ppermute only.
A program may use at most 64 MiB of HBM per device.

v0:
```python
import jax
import jax.numpy as jnp
from jax import lax
from jax.sharding import PartitionSpec as P

BS = 512
HD = 128
GROUP = 8


def as_sent(x):
    return jax.tree.map(lambda a: a.astype(jnp.bfloat16) if a.dtype == jnp.float32 else a, x)


def local(queries, keys, values, chosen):
    scale = HD ** (-0.5)
    blk_count = lax.axis_size("blk")
    rank = lax.axis_index("blk")
    head = lax.axis_index("uly")
    tok = queries.shape[0]
    kv_heads = keys.shape[1] // HD
    q_split = queries.reshape(tok, kv_heads, GROUP * HD)
    kv_split = jnp.concatenate(
        [keys.reshape(tok, kv_heads, HD), values.reshape(tok, kv_heads, HD)], axis=2
    )
    q_head, kv_head = (
        lax.all_to_all(q_split, "uly", split_axis=1, concat_axis=0, tiled=True),
        lax.all_to_all(kv_split, "uly", split_axis=1, concat_axis=0, tiled=True),
    )
    span = q_head.shape[0]
    blocks_here = span // BS
    pieces = BS // blk_count
    spread = lax.all_to_all(
        kv_head.reshape(1, blocks_here, blk_count, pieces, 2 * HD),
        "blk",
        split_axis=2,
        concat_axis=0,
        tiled=True,
    )
    table = spread.reshape(blk_count * blocks_here, pieces, 2 * HD)
    wanted = lax.dynamic_index_in_dim(chosen, head, 1, keepdims=False)
    own_ids = lax.dynamic_slice_in_dim(wanted, rank * blocks_here, blocks_here, 0)
    block_ids = rank * blocks_here + jnp.arange(blocks_here, dtype=jnp.int32)
    usable = own_ids < block_ids[:, None]
    q_blocks = q_head.reshape(blocks_here, BS, GROUP, HD)
    own_rows = kv_head.reshape(blocks_here, BS, 2 * HD)
    causal = jnp.arange(BS, dtype=jnp.int32)[None, :] <= jnp.arange(BS, dtype=jnp.int32)[:, None]
    items = jnp.arange(blocks_here * GROUP, dtype=jnp.int32)
    contract = (((1,), (1,)), ((), ()))

    def query_of(item):
        block_q = lax.dynamic_index_in_dim(q_blocks, item // GROUP, 0, keepdims=False)
        return lax.dynamic_index_in_dim(block_q, item % GROUP, 1, keepdims=False)

    def own_part(item):
        query_rows = query_of(item)
        kv_rows = lax.dynamic_index_in_dim(own_rows, item // GROUP, 0, keepdims=False)
        scores = (
            lax.dot_general(
                query_rows, kv_rows[:, :HD], contract, preferred_element_type=jnp.float32
            )
            * scale
        )
        return jnp.where(causal, scores, -jnp.inf)

    def finish(item, own_scores, picked):
        index = item // GROUP
        query_rows = query_of(item)
        own_kv = lax.dynamic_index_in_dim(own_rows, index, 0, keepdims=False)
        routed_kv = lax.dynamic_index_in_dim(picked, index, 0, keepdims=False)
        allowed = lax.dynamic_index_in_dim(usable, index, 0, keepdims=False)
        routed_scores = (
            lax.dot_general(
                query_rows, routed_kv[:, :HD], contract, preferred_element_type=jnp.float32
            )
            * scale
        )
        routed_mask = jnp.repeat(allowed, BS, total_repeat_length=2 * BS)[None, :]
        routed_scores = jnp.where(routed_mask, routed_scores, -jnp.inf)
        top = jnp.maximum(jnp.max(own_scores, axis=-1), jnp.max(routed_scores, axis=-1))[:, None]
        own_weights = jnp.exp(own_scores - top)
        routed_weights = jnp.exp(routed_scores - top)
        total = jnp.sum(own_weights, axis=-1) + jnp.sum(routed_weights, axis=-1)
        summed = jnp.dot(
            own_weights.astype(jnp.bfloat16), own_kv[:, HD:], preferred_element_type=jnp.float32
        )
        summed = summed + jnp.dot(
            routed_weights.astype(jnp.bfloat16),
            routed_kv[:, HD:],
            preferred_element_type=jnp.float32,
        )
        return (summed / total[:, None]).astype(jnp.bfloat16)

    request = table[wanted.reshape(-1)].reshape(blk_count, blocks_here * 2, 1, pieces, 2 * HD)
    arrived = lax.all_to_all(request, "blk", split_axis=0, concat_axis=2, tiled=True)
    picked = arrived.reshape(blocks_here, 2 * BS, 2 * HD)

    def with_late(item):
        return finish(item, own_part(item), picked)

    result = lax.map(with_late, items)
    gathered = (
        result.reshape(blocks_here, GROUP, BS, HD)
        .transpose(0, 2, 1, 3)
        .reshape(span, 1, GROUP * HD)
    )
    returned = lax.all_to_all(
        as_sent(gathered), "uly", split_axis=0, concat_axis=1, tiled=True
    ).astype(gathered.dtype)
    return returned.reshape(tok, kv_heads * GROUP * HD)


def solution(mesh):
    placed = (P(("blk", "uly"), None), P(("blk", "uly"), None), P(("blk", "uly"), None), P())
    return jax.shard_map(
        local, mesh=mesh, in_specs=placed, out_specs=P(("blk", "uly"), None), check_vma=False
    )
```

profile of v0, /device:TPU:0, one launch (start us, length us, event | category | flops | bytes accessed | tf_op | source)
XLA Modules:
  0.0 357.1 jit_solution(6223399232860160426)
XLA Ops:
  2.3 12.0 %all_to_all.75 = bf16[512,2,256]{0,2,1:T(8,128)(2,1)S(1)} all-to-all(bf16[512,2,256]{0,2,1:T(8,128)(2,1)S(1)} %pad_maximum_fusion), channel_id=1, replica_groups=mesh['blk'=16,'uly'=2] {'uly'}, dimensions={1} | all-to-all | bytes 1048576 | tf_op jit(solution)/shard_map/all_to_all | solution.py:28
  15.3 6.0 %all-to-all-start.2 = ((bf16[1,2,16,32,256]{4,3,1,0,2:T(8,128)(2,1)}), bf16[1,2,16,32,256]{4,3,1,0,2:T(8,128)(2,1)S(1)}, u32[]{:S(2)}, u32[]{:S(2)}) async-start(bf16[1,2,16,32,256]{4,3,1,0,2:T(8,128)(2,1)} %copy.33), calls=%async_computation.2 | async-start | bytes 1048576 | tf_op jit(solution)/shard_map/all_to_all | solution.py:33
  21.6 14.2 %all-to-all-done.2 = bf16[1,2,16,32,256]{4,3,1,0,2:T(8,128)(2,1)S(1)} async-done(((bf16[1,2,16,32,256]{4,3,1,0,2:T(8,128)(2,1)}), bf16[1,2,16,32,256]{4,3,1,0,2:T(8,128)(2,1)S(1)}, u32[]{:S(2)}, u32[]{:S(2)}) %all-to-all-start.2) | async-done | bytes 524320 | tf_op jit(solution)/shard_map/all_to_all | solution.py:33
  35.8 1.6 gather_fusion
  37.4 4.1 %all-to-all-start.3 = ((bf16[16,4,1,32,256]{4,3,1,2,0:T(8,128)(2,1)}), bf16[16,4,1,32,256]{4,3,1,2,0:T(8,128)(2,1)S(1)}, u32[]{:S(2)}, u32[]{:S(2)}) async-start(bf16[16,4,1,32,256]{4,3,1,2,0:T(8,128)(2,1)} %bitcast.17), calls=%async_computation.3 | async-start | bytes 2097152 | tf_op jit(solution)/shard_map/all_to_all | solution.py:95
  41.5 3.9 %copy.28 = bf16[512,2048]{0,1:T(8,128)(2,1)} copy(bf16[512,2048]{1,0:T(8,128)(2,1)} %param.8) | data formatting | bytes 4194304 | tf_op args[0]
  45.4 19.0 %all-to-all-done.3 = bf16[16,4,1,32,256]{4,3,1,2,0:T(8,128)(2,1)S(1)} async-done(((bf16[16,4,1,32,256]{4,3,1,2,0:T(8,128)(2,1)}), bf16[16,4,1,32,256]{4,3,1,2,0:T(8,128)(2,1)S(1)}, u32[]{:S(2)}, u32[]{:S(2)}) %all-to-all-start.3) | async-done | bytes 1048608 | tf_op jit(solution)/shard_map/all_to_all | solution.py:95
  64.4 4.8 %all-to-all-start = ((bf16[512,2,1024]{0,2,1:T(8,128)(2,1)}), bf16[512,2,1024]{0,2,1:T(8,128)(2,1)}, u32[]{:S(2)}, u32[]{:S(2)}) async-start(bf16[512,2,1024]{0,2,1:T(8,128)(2,1)} %bitcast), calls=%async_computation | async-start | bytes 4194304 | tf_op jit(solution)/shard_map/all_to_all | solution.py:27
  70.6 24.6 %all-to-all-done = bf16[512,2,1024]{0,2,1:T(8,128)(2,1)} async-done(((bf16[512,2,1024]{0,2,1:T(8,128)(2,1)}), bf16[512,2,1024]{0,2,1:T(8,128)(2,1)}, u32[]{:S(2)}, u32[]{:S(2)}) %all-to-all-start) | async-done | bytes 2097184 | tf_op jit(solution)/shard_map/all_to_all | solution.py:27
  95.2 195.4 %while.17 = (s32[]{:T(128)}, bf16[16,512,128]{2,1,0:T(8,128)(2,1)}, s32[16]{0:T(128)S(1)}, bf16[2,512,8,128]{1,3,2,0:T(8,128)(2,1)}, bf16[2,512,256]{1,2,0:T(8,1...) while((s32[]{:T(128)}, bf16[16,512,128]{2,1,0:T(8,128)(2,1)}, ...), condition=%wide.region_5.6_spmd.clone, body=%wide.region_0.5_spmd.clone.sunk | while | flops 410714144 | bytes 14323206 | solution.py:101
  101.3 1.5 fusion.49
  113.5 1.5 fusion.49
  150.1 1.5 fusion.49
  235.6 1.5 fusion.49
  272.2 1.5 fusion.49
  290.6 2.9 copy.47
  293.5 6.2 %reshape.271 = bf16[1024,1,1024]{2,1,0:T(2,128)(2,1)} reshape(bf16[2,512,8,128]{3,2,1,0:T(8,128)(2,1)S(1)} %bitcast.82) | data formatting | bytes 4194304 | tf_op jit(solution)/shard_map/reshape | solution.py:105
  300.3 12.8 %reduce.2 = bf16[1024,1024]{1,0:T(8,128)(2,1)S(1)} reduce(bf16[1024,1,1024]{2,1,0:T(2,128)(2,1)} %reshape.271, bf16[]{:T(256)} %broadcast.234), dimensions={1}, to_apply=%reshape.271.reduce_sub_computation | reduce | bytes 4194306 | tf_op jit(solution)/shard_map/reshape | solution.py:105
  313.0 2.5 reshape.272
  315.6 29.0 %all_to_all.76 = bf16[2,2,262144]{2,1,0:T(2,128)(2,1)S(1)} all-to-all(bf16[2,2,262144]{2,1,0:T(2,128)(2,1)} %reshape.272), channel_id=1, replica_groups=mesh['blk'=16,'uly'=2] {'uly'}, dimensions={0} | all-to-all | bytes 4194304 | tf_op jit(solution)/shard_map/all_to_all | solution.py:107
  344.5 3.1 reshape.273
  347.6 3.0 copy.45
  350.6 2.6 copy.41
  353.2 3.9 %copy.42 = bf16[512,2048]{1,0:T(8,128)(2,1)} copy(bf16[512,2048]{0,1:T(8,128)(2,1)} %bitcast.84) | data formatting | bytes 4194304 | tf_op jit(solution)/shard_map/reshape | solution.py:110
  (289 shorter events, 152.4 us)
Async XLA Ops:
  0.0 21.3 %copy-start = (s32[32,2,2]{0,2,1:T(2,128)S(1)}, s32[32,2,2]{0,2,1:T(2,128)}, u32[]{:S(2)}) copy-start(s32[32,2,2]{0,2,1:T(2,128)} %param.11) | copy-start | bytes 1540
  15.3 20.5 %all-to-all-start.2 = ((bf16[1,2,16,32,256]{4,3,1,0,2:T(8,128)(2,1)}), bf16[1,2,16,32,256]{4,3,1,0,2:T(8,128)(2,1)S(1)}, u32[]{:S(2)}, u32[]{:S(2)}) async-start(bf16[1,2,16,32,256]{4,3,1,0,2:T(8,128)(2,1)} %copy.33), calls=%async_computation.2 | async-start | bytes 1048576 | tf_op jit(solution)/shard_map/all_to_all | solution.py:33
  37.4 27.0 %all-to-all-start.3 = ((bf16[16,4,1,32,256]{4,3,1,2,0:T(8,128)(2,1)}), bf16[16,4,1,32,256]{4,3,1,2,0:T(8,128)(2,1)S(1)}, u32[]{:S(2)}, u32[]{:S(2)}) async-start(bf16[16,4,1,32,256]{4,3,1,2,0:T(8,128)(2,1)} %bitcast.17), calls=%async_computation.3 | async-start | bytes 2097152 | tf_op jit(solution)/shard_map/all_to_all | solution.py:95
  64.4 30.8 %all-to-all-start = ((bf16[512,2,1024]{0,2,1:T(8,128)(2,1)}), bf16[512,2,1024]{0,2,1:T(8,128)(2,1)}, u32[]{:S(2)}, u32[]{:S(2)}) async-start(bf16[512,2,1024]{0,2,1:T(8,128)(2,1)} %bitcast), calls=%async_computation | async-start | bytes 4194304 | tf_op jit(solution)/shard_map/all_to_all | solution.py:27
  69.3 26.0 %copy-start.2 = (pred[1024]{0:T(1024)(128)(4,1)S(1)}, pred[1024]{0:T(1024)(128)(4,1)}, u32[]{:S(2)}) copy-start(pred[1024]{0:T(1024)(128)(4,1)} %constant.389) | copy-start | bytes 3076
  105.5 1.0 copy-start.1
  117.7 1.0 copy-start.1
  129.9 1.0 copy-start.1
  142.1 1.0 copy-start.1
  154.3 1.0 copy-start.1
  166.5 1.0 copy-start.1
  178.7 1.0 copy-start.1
  190.9 1.0 copy-start.1
  203.2 1.0 copy-start.1
  215.4 1.0 copy-start.1
  227.6 1.0 copy-start.1
  239.8 1.0 copy-start.1
  252.0 1.0 copy-start.1
  264.2 1.0 copy-start.1
  276.4 1.0 copy-start.1
  288.6 1.0 copy-start.1
where the time goes:
time: 361 us; the launch traced here: 357 us
  local copies, waits for them, and re-layouts  88 us (24%)
  matrix products  68.9 us (19%)
  waiting for transfers between devices  57.8 us (16%)
  other arithmetic  45.2 us (13%)
  loops' own time  41.1 us (11%)
  blocking collectives  41 us (11%)
  starting transfers between devices  14.9 us (4%)
    another operation x1, loops' own time, local(): result = lax.map(with_late, items)  41.1 us
    all_to_all x1, blocking collectives, local(): lax.all_to_all(as_sent(gathered), 'uly', split_axis=0, concat_axis=1, til...  29 us
    all_to_all x1, waiting for transfers between devices, local(): lax.all_to_all(q_split, 'uly', split_axis=1, concat_axis=0, tiled=True)  24.6 us
    dot_general x16, matrix products, finish(): lax.dot_general(query_rows, routed_kv[:, :HD], contract, preferred_elemen...  23.2 us
    dot_general x16, matrix products, own_part(): lax.dot_general(query_rows, kv_rows[:, :HD], contract, preferred_element_...  20.2 us
    gather x16, other arithmetic, finish(): routed_mask = jnp.repeat(allowed, BS, total_repeat_length=2 * BS)[None, :]  19.6 us
    all_to_all x1, waiting for transfers between devices, local(): lax.all_to_all(request, 'blk', split_axis=0, concat_axis=2, tiled=True)  19 us
    squeeze x16, local copies, waits for them, and re-layouts, finish(): routed_kv = lax.dynamic_index_in_dim(picked, index, 0, keepdims=False)  17.3 us
  transfers between devices with their start and end apart: 3, of which 3 were waited for; matrix products, arithmetic and copies ran while one was open for 2% of the time, Pallas kernels for 0%

commit v1 on v0

--- a/solution.py
+++ b/solution.py
@@ -1,18 +1,130 @@
+import functools
+import math
+
 import jax
 import jax.numpy as jnp
 from jax import lax
+from jax.experimental import pallas as pl
+from jax.experimental.pallas import tpu as pltpu
 from jax.sharding import PartitionSpec as P
 
 BS = 512
 HD = 128
 GROUP = 8
+AXES = ("blk", "uly")
+TILE = 256
+HEADS_A_STEP = 4
+EXPONENT = HD ** (-0.5) * math.log2(math.e)
+
+
+def scores_of(rows, key_rows):
+    return lax.dot_general(
+        rows, key_rows, (((1,), (1,)), ((), ())), preferred_element_type=jnp.float32
+    )
+
+
+def lane_max(scores):
+    parts = [scores[:, i : i + HD] for i in range(0, scores.shape[1], HD)]
+    return functools.reduce(jnp.maximum, parts)
+
+
+def attend_kernel(usable, q_ref, k_ref, v_ref, routed_ref, out_ref):
+    head = pl.program_id(0) * HEADS_A_STEP // GROUP
+    use = [usable[head, s] != 0 for s in range(2)]
+    ones = jnp.ones((BS, HD), jnp.bfloat16)
+    own_k = k_ref[...]
+    own_v = jnp.concatenate([v_ref[...], ones], axis=1)
+    routed_k = [routed_ref[:, s, :, :HD].reshape(BS, HD) for s in range(2)]
+    routed_v = [
+        jnp.concatenate([routed_ref[:, s, :, HD:].reshape(BS, HD), ones], axis=1) for s in range(2)
+    ]
+    causal = lax.broadcasted_iota(jnp.int32, (TILE, TILE), 1) <= lax.broadcasted_iota(
+        jnp.int32, (TILE, TILE), 0
+    )
+
+    def first(item):
+        col, start = item
+        rows = q_ref[start : start + TILE, col : col + HD]
+        return scores_of(rows, own_k[: start + TILE]), [scores_of(rows, k) for k in routed_k]
+
+    def second(item, scored):
+        col, start = item
+        own, routed = scored
+        diagonal = jnp.where(causal, own[:, start:], -jnp.inf)
+        own = jnp.concatenate([own[:, :start], diagonal], axis=1) if start else diagonal
+        top = lane_max(own)
+        for s in range(2):
+            top = jnp.maximum(top, jnp.where(use[s], lane_max(routed[s]), -jnp.inf))
+        top = jnp.max(top, axis=1, keepdims=True) * EXPONENT
+        weights = jnp.exp2(own * EXPONENT - top).astype(jnp.bfloat16)
+        both = jnp.dot(weights, own_v[: start + TILE], preferred_element_type=jnp.float32)
+        for s in range(2):
+            bound = jnp.where(use[s], top, jnp.inf)
+            weights = jnp.exp2(routed[s] * EXPONENT - bound).astype(jnp.bfloat16)
+            both = both + jnp.dot(weights, routed_v[s], preferred_element_type=jnp.float32)
+        out_ref[start : start + TILE, col : col + HD] = (both[:, :HD] / both[:, HD:]).astype(
+            out_ref.dtype
+        )
+
+    items = [(h * HD, t) for h in range(HEADS_A_STEP) for t in range(0, BS, TILE)]
+    held = first(items[0])
+    for item, following in zip(items, items[1:] + [None]):
+        ahead = first(following) if following else None
+        second(item, held)
+        held = ahead
+
+
+def attend(usable, queries, keys, values, routed):
+    heads = queries.shape[1] // HD
+    shares, rows = routed.shape[0], routed.shape[2]
+    step = HEADS_A_STEP
+    return pl.pallas_call(
+        attend_kernel,
+        grid_spec=pltpu.PrefetchScalarGridSpec(
+            num_scalar_prefetch=1,
+            grid=(heads // step,),
+            in_specs=[
+                pl.BlockSpec((BS, step * HD), lambda i, u: (0, i)),
+                pl.BlockSpec((BS, HD), lambda i, u: (0, i * step // GROUP)),
+                pl.BlockSpec((BS, HD), lambda i, u: (0, i * step // GROUP)),
+                pl.BlockSpec((shares, 2, rows, 2 * HD), lambda i, u: (0, i * step // GROUP, 0, 0)),
+            ],
+            out_specs=pl.BlockSpec((BS, step * HD), lambda i, u: (0, i)),
+        ),
+        out_shape=jax.ShapeDtypeStruct(queries.shape, queries.dtype),
+        compiler_params=pltpu.CompilerParams(vmem_limit_bytes=48 * 2**20),
+        cost_estimate=pl.CostEstimate(
+            flops=4 * BS * 3 * BS * HD * heads,
+            bytes_accessed=4 * queries.size + 8 * keys.size,
+            transcendentals=BS * 3 * BS * heads,
+        ),
+        name="attend",
+    )(usable, queries, keys, values, routed)
+
+
+def resident(queries, keys, values, chosen):
+    count = lax.axis_size(AXES)
+    me = lax.axis_index(AXES)
+    kv_heads = keys.shape[1] // HD
+    rows = BS // count
+    pairs = jnp.concatenate(
+        [keys.reshape(count, rows, kv_heads, HD), values.reshape(count, rows, kv_heads, HD)], axis=3
+    )
+    shared = lax.all_to_all(pairs.transpose(0, 2, 1, 3), AXES, 0, 0, tiled=True)
+    table = shared.reshape(count * kv_heads, rows, 2 * HD)
+    wanted = chosen * kv_heads + jnp.arange(kv_heads, dtype=jnp.int32)[None, :, None]
+    request = table[wanted.reshape(-1)].reshape(count, kv_heads * 2, rows, 2 * HD)
+    routed = lax.all_to_all(request, AXES, 0, 0, tiled=True)
+    own_ids = lax.dynamic_index_in_dim(chosen, me, 0, keepdims=False)
+    usable = (own_ids < me).astype(jnp.int32)
+    return attend(usable, queries, keys, values, routed)
 
 
 def as_sent(x):
     return jax.tree.map(lambda a: a.astype(jnp.bfloat16) if a.dtype == jnp.float32 else a, x)
 
 
-def local(queries, keys, values, chosen):
+def split_heads(queries, keys, values, chosen):
     scale = HD ** (-0.5)
     blk_count = lax.axis_size("blk")
     rank = lax.axis_index("blk")
@@ -110,6 +222,13 @@
     return returned.reshape(tok, kv_heads * GROUP * HD)
 
 
+def local(queries, keys, values, chosen):
+    count = lax.axis_size(AXES)
+    if queries.shape[0] == BS and BS % (16 * count) == 0:
+        return resident(queries, keys, values, chosen)
+    return split_heads(queries, keys, values, chosen)
+
+
 def solution(mesh):
     placed = (P(("blk", "uly"), None), P(("blk", "uly"), None), P(("blk", "uly"), None), P())
     return jax.shard_map(

time: 361 us -> 77.5 us (0.21)
  local copies, waits for them, and re-layouts: 88 us -> 5.61 us
  matrix products: 68.9 us -> 0 us
  other arithmetic: 45.2 us -> 1.71 us
  loops' own time: 41.1 us -> 0 us
  blocking collectives: 41 us -> 0 us
  Pallas kernels: 0 us -> 18.1 us
  waiting for transfers between devices: 57.8 us -> 40.7 us
  starting transfers between devices: 14.9 us -> 10.9 us
    dot_general x64 -> x0, matrix products: 68.9 us -> none  [the longest x16 23.2 us: finish(): lax.dot_general(query_rows, routed_kv[:, :HD], contract, preferred_elemen...]
    another operation x1 -> x0, loops' own time: 41.1 us -> none  [local(): result = lax.map(with_late, items)]
    all_to_all x2 -> x0, blocking collectives: 41 us -> none  [the longest x1 29 us: local(): lax.all_to_all(as_sent(gathered), 'uly', split_axis=0, concat_axis=1, til...]
    dynamic_slice x68 -> x0, local copies, waits for them, and re-layouts: 24 us -> none  [the longest x32 14.2 us: own_part(): lax.dynamic_index_in_dim(own_rows, item // GROUP, 0, keepdims=False)]
    gather x17 -> x1, other arithmetic: 19.6 us -> 0.01 us  [resident(): table[wanted.reshape(-1)].reshape(count, kv_heads * 2, rows, 2 * HD)]
    pallas_call x0 -> x1, Pallas kernels: none -> 18.1 us  [attend(): pl.pallas_call(attend_kernel, grid_spec=pltpu.PrefetchScalarGridSpec(num_...]
    squeeze x16 -> x0, local copies, waits for them, and re-layouts: 17.3 us -> none  [finish(): routed_kv = lax.dynamic_index_in_dim(picked, index, 0, keepdims=False)]
    all_to_all x3 -> x2, waiting for transfers between devices: 57.8 us -> 40.7 us  [the longest x1 26 us: resident(): routed = lax.all_to_all(request, AXES, 0, 0, tiled=True)]
  transfers between devices with their start and end apart: 3 -> 2, of which waited for: 3 -> 2; matrix products, arithmetic and copies ran while one was open for 2% -> 1% of each run, Pallas kernels for 0% -> 0%
where the time goes in v1:
time: 77.5 us; the launch traced here: 77.1 us
  waiting for transfers between devices  40.7 us (53%)
  Pallas kernels  18.1 us (23%)
  starting transfers between devices  10.9 us (14%)
  local copies, waits for them, and re-layouts  5.61 us (7%)
  other arithmetic  1.71 us (2%)
    all_to_all x1, waiting for transfers between devices, resident(): routed = lax.all_to_all(request, AXES, 0, 0, tiled=True)  26 us
    pallas_call x1, Pallas kernels, attend(): pl.pallas_call(attend_kernel, grid_spec=pltpu.PrefetchScalarGridSpec(num_...  18.1 us
    all_to_all x1, waiting for transfers between devices, resident(): shared = lax.all_to_all(pairs.transpose(0, 2, 1, 3), AXES, 0, 0, tiled=True)  14.7 us
    all_to_all x1, starting transfers between devices, resident(): shared = lax.all_to_all(pairs.transpose(0, 2, 1, 3), AXES, 0, 0, tiled=True)  7.3 us
    all_to_all x1, starting transfers between devices, resident(): routed = lax.all_to_all(request, AXES, 0, 0, tiled=True)  3.62 us
    gather x1, local copies, waits for them, and re-layouts, resident(): table[wanted.reshape(-1)].reshape(count, kv_heads * 2, rows, 2 * HD)  1.61 us
    unnamed x8, local copies, waits for them, and re-layouts  1.61 us
  transfers between devices with their start and end apart: 2, of which 2 were waited for; matrix products, arithmetic and copies ran while one was open for 1% of the time, Pallas kernels for 0%

profile of v1, /device:TPU:0, one launch (start us, length us, event | category | flops | bytes accessed | tf_op | source)
XLA Modules:
  0.0 77.1 jit_solution(7528840950038127026)
XLA Ops:
  0.0 0.0 copy-start.3
  0.0 1.0 %reshape.47 = bf16[32,16,2,128]{3,2,1,0:T(2,128)(2,1)S(1)} reshape(bf16[512,256]{1,0:T(8,128)(2,1)} %k_ref.1) | data formatting | bytes 524288 | tf_op jit(solution)/shard_map/reshape | solution.py:111
  1.0 1.0 %reshape.48 = bf16[32,16,2,128]{3,2,1,0:T(2,128)(2,1)S(1)} reshape(bf16[512,256]{1,0:T(8,128)(2,1)} %v_ref.1) | data formatting | bytes 524288 | tf_op jit(solution)/shard_map/reshape | solution.py:111
  2.1 1.5 %maximum_bitcast_fusion = bf16[32,2,16,256]{3,1,2,0:T(2,128)(2,1)} fusion(bf16[32,16,2,128]{3,2,1,0:T(2,128)(2,1)S(1)} %reshape.48, bf16[32,16,2,128]{3,2,1,0:T(2,128)(2,1)S(1)} %reshape.47), kind=kLoop, calls=%fused_computation.1 | loop fusion | flops 1048576 | bytes 1048576 | tf_op jit(solution)/shard_map/transpose | solution.py:113
  3.5 7.3 %all-to-all-start = ((bf16[32,2,16,256]{3,1,2,0:T(2,128)(2,1)}), bf16[32,2,16,256]{3,1,2,0:T(2,128)(2,1)S(1)}, u32[]{:S(2)}, u32[]{:S(2)}) async-start(bf16[32,2,16,256]{3,1,2,0:T(2,128)(2,1)} %maximum_bitcast_fusion), calls=%async_computation | async-start | bytes 1048576 | tf_op jit(solution)/shard_map/all_to_all | solution.py:113
  10.8 0.0 copy-done.3
  10.9 0.1 copy.8
  11.0 0.1 reshape.50
  11.1 14.7 %all-to-all-done = bf16[32,2,16,256]{3,1,2,0:T(2,128)(2,1)S(1)} async-done(((bf16[32,2,16,256]{3,1,2,0:T(2,128)(2,1)}), bf16[32,2,16,256]{3,1,2,0:T(2,128)(2,1)S(1)}, u32[]{:S(2)}, u32[]{:S(2)}) %all-to-all-start) | async-done | bytes 524320 | tf_op jit(solution)/shard_map/all_to_all | solution.py:113
  25.8 0.1 copy.7
  25.9 0.0 copy-start
  26.0 0.0 copy-start.1
  26.0 1.6 %gather_fusion = bf16[128,16,256]{2,1,0:T(8,128)(2,1)} fusion(bf16[64,16,256]{2,1,0:T(8,128)(2,1)S(1)} %bitcast.6, s32[1024]{0:T(1024)S(1)} %pad_clamp_fusion), kind=kCustom, calls=%fused_computation | custom fusion | bytes 2097664 | tf_op jit(solution)/shard_map/gather | solution.py:116
  27.6 3.6 %all-to-all-start.1 = ((bf16[32,4,16,256]{3,2,1,0:T(8,128)(2,1)}), bf16[32,4,16,256]{3,2,1,0:T(8,128)(2,1)S(1)}, u32[]{:S(2)}, u32[]{:S(2)}) async-start(bf16[32,4,16,256]{3,2,1,0:T(8,128)(2,1)} %bitcast.3), calls=%async_computation.1 | async-start | bytes 2097152 | tf_op jit(solution)/shard_map/all_to_all | solution.py:117
  31.2 0.2 fusion.usable
  31.4 26.0 %all-to-all-done.1.routed_ref = bf16[32,4,16,256]{3,2,1,0:T(8,128)(2,1)S(1)} async-done(((bf16[32,4,16,256]{3,2,1,0:T(8,128)(2,1)}), bf16[32,4,16,256]{3,2,1,0:T(8,128)(2,1)S(1)}, u32[]{:S(2)}, u32[]{:S(2)}) %all-to-all-start.1) | async-done | bytes 1048608 | tf_op jit(solution)/shard_map/all_to_all | solution.py:117
  57.4 0.0 copy-done
  57.4 0.0 copy-done.1
  57.4 0.0 copy-start.2
  57.5 1.6 %copy-done.2 = bf16[512,2048]{1,0:T(8,128)(2,1)S(1)} copy-done((bf16[512,2048]{1,0:T(8,128)(2,1)S(1)}, bf16[512,2048]{1,0:T(8,128)(2,1)}, u32[]{:S(2)}) %copy-start.2) | copy-done | bytes 2097176
  59.0 18.1 %attend.1 = bf16[512,2048]{1,0:T(8,128)(2,1)} custom-call(s32[2,2]{1,0:T(2,128)S(1)} %fusion.usable, bf16[512,2048]{1,0:T(8,128)(2,1)S(1)} %copy-done.2, bf16[512,256]{1,0:T(8,128)(2,1)S(1)} %copy-done, bf16[512,256]{1,0:T(8,128)(2,1)S(1)} %copy-done.1, bf16[32,4,16,256]{3,2,1,0:T(8,128)(2,1)S(1)} %all-to-all-done.1.routed_ref), custom_call_target="tpu_custom_call" | custom-call | flops 6442450944 | bytes 5242880 | tf_op jit(solution)/shard_map/attend/pallas_call | solution.py:81
  (3 shorter events, 0.0 us)
Async XLA Ops:
  0.0 10.8 %copy-start.3 = (s32[32,2,2]{0,2,1:T(2,128)S(1)}, s32[32,2,2]{0,2,1:T(2,128)}, u32[]{:S(2)}) copy-start(s32[32,2,2]{0,2,1:T(2,128)} %param.7) | copy-start | bytes 1540
  3.5 22.3 %all-to-all-start = ((bf16[32,2,16,256]{3,1,2,0:T(2,128)(2,1)}), bf16[32,2,16,256]{3,1,2,0:T(2,128)(2,1)S(1)}, u32[]{:S(2)}, u32[]{:S(2)}) async-start(bf16[32,2,16,256]{3,1,2,0:T(2,128)(2,1)} %maximum_bitcast_fusion), calls=%async_computation | async-start | bytes 1048576 | tf_op jit(solution)/shard_map/all_to_all | solution.py:113
  25.9 31.5 %copy-start = (bf16[512,256]{1,0:T(8,128)(2,1)S(1)}, bf16[512,256]{1,0:T(8,128)(2,1)}, u32[]{:S(2)}) copy-start(bf16[512,256]{1,0:T(8,128)(2,1)} %k_ref.1) | copy-start | bytes 786436
  26.0 31.5 %copy-start.1 = (bf16[512,256]{1,0:T(8,128)(2,1)S(1)}, bf16[512,256]{1,0:T(8,128)(2,1)}, u32[]{:S(2)}) copy-start(bf16[512,256]{1,0:T(8,128)(2,1)} %v_ref.1) | copy-start | bytes 786436
  27.6 29.9 %all-to-all-start.1 = ((bf16[32,4,16,256]{3,2,1,0:T(8,128)(2,1)}), bf16[32,4,16,256]{3,2,1,0:T(8,128)(2,1)S(1)}, u32[]{:S(2)}, u32[]{:S(2)}) async-start(bf16[32,4,16,256]{3,2,1,0:T(8,128)(2,1)} %bitcast.3), calls=%async_computation.1 | async-start | bytes 2097152 | tf_op jit(solution)/shard_map/all_to_all | solution.py:117
  57.4 1.6 %copy-start.2 = (bf16[512,2048]{1,0:T(8,128)(2,1)S(1)}, bf16[512,2048]{1,0:T(8,128)(2,1)}, u32[]{:S(2)}) copy-start(bf16[512,2048]{1,0:T(8,128)(2,1)} %q_ref.1) | copy-start | bytes 6291460

commit v2 on v0

--- a/solution.py
+++ b/solution.py
@@ -1,18 +1,238 @@
+import functools
+import math
+
 import jax
 import jax.numpy as jnp
 from jax import lax
+from jax.experimental import pallas as pl
+from jax.experimental.pallas import tpu as pltpu
 from jax.sharding import PartitionSpec as P
 
 BS = 512
 HD = 128
 GROUP = 8
+AXES = ("blk", "uly")
+TILE = 256
+STEP = GROUP
+ROOM = 2.0**100
+EXPONENT = HD ** (-0.5) * math.log2(math.e)
+
+
+def scores_of(rows, key_rows):
+    return lax.dot_general(
+        rows, key_rows, (((1,), (1,)), ((), ())), preferred_element_type=jnp.float32
+    )
+
+
+def weighted(scores, top, values):
+    weights = jnp.exp2(scores * EXPONENT - top).astype(jnp.bfloat16)
+    return jnp.dot(weights, values, preferred_element_type=jnp.float32)
+
+
+def lane_max(scores):
+    parts = [scores[:, i : i + HD] for i in range(0, scores.shape[1], HD)]
+    return functools.reduce(jnp.maximum, parts)
+
+
+def staggered(items, first, second):
+    held = first(items[0])
+    for item, following in zip(items, items[1:] + [None]):
+        ahead = first(following) if following else None
+        second(item, held)
+        held = ahead
+
+
+def with_ones(values):
+    return jnp.concatenate([values, jnp.ones_like(values)], axis=1)
+
+
+def own_kernel(q_ref, k_ref, v_ref, sum_ref, stat_ref):
+    keys = k_ref[...]
+    values = with_ones(v_ref[...])
+    shape = (TILE, TILE)
+    causal = lax.broadcasted_iota(jnp.int32, shape, 1) <= lax.broadcasted_iota(jnp.int32, shape, 0)
+    lane = lax.broadcasted_iota(jnp.int32, (TILE, HD), 1)
+    stats = {}
+
+    def first(item):
+        h, start = item
+        rows = q_ref[start : start + TILE, h * HD : (h + 1) * HD]
+        return scores_of(rows, keys[: start + TILE])
+
+    def second(item, scores):
+        h, start = item
+        diagonal = jnp.where(causal, scores[:, start:], -jnp.inf)
+        scores = jnp.concatenate([scores[:, :start], diagonal], axis=1) if start else diagonal
+        top = jnp.max(lane_max(scores), axis=1, keepdims=True) * EXPONENT
+        both = weighted(scores, top, values[: start + TILE])
+        sum_ref[start : start + TILE, h * HD : (h + 1) * HD] = both[:, :HD]
+        stat = stats.get(start, jnp.zeros((TILE, HD), jnp.float32))
+        stat = jnp.where(lane == h, top, stat)
+        stats[start] = jnp.where(lane == STEP + h, both[:, HD:], stat)
+
+    staggered([(h, t) for h in range(STEP) for t in range(0, BS, TILE)], first, second)
+    for start, stat in stats.items():
+        stat_ref[start : start + TILE, :] = stat
+
+
+def attend_own(queries, keys, values):
+    heads = queries.shape[1] // HD
+    return pl.pallas_call(
+        own_kernel,
+        grid=(heads // STEP,),
+        in_specs=[
+            pl.BlockSpec((BS, STEP * HD), lambda i: (0, i)),
+            pl.BlockSpec((BS, HD), lambda i: (0, i * STEP // GROUP)),
+            pl.BlockSpec((BS, HD), lambda i: (0, i * STEP // GROUP)),
+        ],
+        out_specs=[
+            pl.BlockSpec((BS, STEP * HD), lambda i: (0, i)),
+            pl.BlockSpec((BS, HD), lambda i: (0, i)),
+        ],
+        out_shape=[
+            jax.ShapeDtypeStruct(queries.shape, jnp.float32),
+            jax.ShapeDtypeStruct((BS, heads // STEP * HD), jnp.float32),
+        ],
+        compiler_params=pltpu.CompilerParams(vmem_limit_bytes=48 * 2**20),
+        cost_estimate=pl.CostEstimate(
+            flops=3 * BS * BS * HD * heads,
+            bytes_accessed=6 * queries.size,
+            transcendentals=BS * BS * heads,
+        ),
+        name="attend_own",
+    )(queries, keys, values)
+
+
+def routed_kernel(usable, q_ref, first_key_ref, sum_ref, stat_ref, routed_ref, out_ref):
+    kv_head = pl.program_id(0) * STEP // GROUP
+    use = [usable[kv_head, s] != 0 for s in range(2)]
+    none = jnp.zeros((), jnp.bfloat16)
+    ones = jnp.ones((BS, HD), jnp.bfloat16)
+    slots = range(2)
+    keys = jnp.concatenate(
+        [
+            jnp.where(use[s], routed_ref[:, s, :, :HD].reshape(BS, HD), first_key_ref[0:1, :])
+            for s in slots
+        ],
+        axis=0,
+    )
+    values = jnp.concatenate(
+        [
+            jnp.concatenate(
+                [
+                    jnp.where(use[s], routed_ref[:, s, :, HD:].reshape(BS, HD), none),
+                    jnp.where(use[s], ones, none),
+                ],
+                axis=1,
+            )
+            for s in slots
+        ],
+        axis=0,
+    )
+    seen = []
+
+    def first(item):
+        h, start = item
+        return scores_of(q_ref[start : start + TILE, h * HD : (h + 1) * HD], keys)
+
+    def second(item, scores):
+        h, start = item
+        here = slice(start, start + TILE), slice(h * HD, (h + 1) * HD)
+        own_top = stat_ref[start : start + TILE, h : h + 1]
+        own_total = stat_ref[start : start + TILE, STEP + h : STEP + h + 1]
+        both = weighted(scores, own_top, values)
+        total = both[:, HD:] + own_total
+        seen.append(total)
+        out_ref[here] = ((both[:, :HD] + sum_ref[here]) / total).astype(out_ref.dtype)
+
+    staggered([(h, t) for h in range(STEP) for t in range(0, BS, TILE)], first, second)
+    in_range = functools.reduce(jnp.logical_and, [total < ROOM for total in seen])
+
+    @pl.when(jnp.logical_not(jnp.all(in_range)))
+    def _():
+        lane = lax.broadcasted_iota(jnp.int32, (TILE, HD), 1)
+
+        @pl.loop(0, STEP * (BS // TILE))
+        def _(item):
+            h = item // (BS // TILE)
+            rows = pl.ds(pl.multiple_of(item % (BS // TILE) * TILE, TILE), TILE)
+            here = rows, pl.ds(pl.multiple_of(h * HD, HD), HD)
+            stat = stat_ref[rows, :]
+            own_top = jnp.sum(jnp.where(lane == h, stat, 0.0), axis=1, keepdims=True)
+            own_total = jnp.sum(jnp.where(lane == STEP + h, stat, 0.0), axis=1, keepdims=True)
+            scores = scores_of(q_ref[here], keys)
+            top = jnp.max(lane_max(scores), axis=1, keepdims=True) * EXPONENT
+            top = jnp.maximum(top, own_top)
+            scale = jnp.exp2(own_top - top)
+            both = weighted(scores, top, values)
+            total = both[:, HD:] + own_total * scale
+            out_ref[here] = ((both[:, :HD] + sum_ref[here] * scale) / total).astype(out_ref.dtype)
+
+
+def attend_routed(usable, queries, keys, own_sum, own_stat, routed):
+    shares, _, rows, _ = routed.shape
+    heads = queries.shape[1] // HD
+    here = lambda i, u: (0, i)
+    return pl.pallas_call(
+        routed_kernel,
+        grid_spec=pltpu.PrefetchScalarGridSpec(
+            num_scalar_prefetch=1,
+            grid=(heads // STEP,),
+            in_specs=[
+                pl.BlockSpec((BS, STEP * HD), here),
+                pl.BlockSpec((16, HD), lambda i, u: (0, i * STEP // GROUP)),
+                pl.BlockSpec((BS, STEP * HD), here),
+                pl.BlockSpec((BS, HD), here),
+                pl.BlockSpec((shares, 2, rows, 2 * HD), lambda i, u: (0, i * STEP // GROUP, 0, 0)),
+            ],
+            out_specs=pl.BlockSpec((BS, STEP * HD), here),
+        ),
+        out_shape=jax.ShapeDtypeStruct(queries.shape, queries.dtype),
+        compiler_params=pltpu.CompilerParams(vmem_limit_bytes=48 * 2**20),
+        cost_estimate=pl.CostEstimate(
+            flops=8 * BS * BS * HD * heads,
+            bytes_accessed=8 * BS * heads * HD + 2 * routed.size,
+            transcendentals=2 * BS * BS * heads,
+        ),
+        name="attend_routed",
+    )(usable, queries, keys, own_sum, own_stat, routed)
+
+
+def pack_kernel(k_ref, v_ref, out_ref):
+    shares, heads, rows, _ = out_ref.shape
+    for h in range(heads):
+        part = slice(h * HD, (h + 1) * HD)
+        out_ref[:, h, :, :HD] = k_ref[:, part].reshape(shares, rows, HD)
+        out_ref[:, h, :, HD:] = v_ref[:, part].reshape(shares, rows, HD)
+
+
+def pack(keys, values, shares):
+    shape = (shares, keys.shape[1] // HD, BS // shares, 2 * HD)
+    return pl.pallas_call(
+        pack_kernel, out_shape=jax.ShapeDtypeStruct(shape, keys.dtype), name="pack"
+    )(keys, values)
+
+
+def resident(queries, keys, values, chosen):
+    count = lax.axis_size(AXES)
+    me = lax.axis_index(AXES)
+    kv_heads = keys.shape[1] // HD
+    usable = (lax.dynamic_index_in_dim(chosen, me, 0, keepdims=False) < me).astype(jnp.int32)
+    wanted = chosen * kv_heads + jnp.arange(kv_heads, dtype=jnp.int32)[None, :, None]
+    table = lax.all_to_all(pack(keys, values, count), AXES, 0, 0, tiled=True)
+    table = table.reshape(count * kv_heads, BS // count, 2 * HD)
+    own_sum, own_stat = attend_own(queries, keys, values)
+    wanted, own_stat = lax.optimization_barrier((wanted.reshape(-1), own_stat))
+    request = table[wanted].reshape(count, kv_heads * 2, BS // count, 2 * HD)
+    routed = lax.all_to_all(request, AXES, 0, 0, tiled=True)
+    return attend_routed(usable, queries, keys, own_sum, own_stat, routed)
 
 
 def as_sent(x):
     return jax.tree.map(lambda a: a.astype(jnp.bfloat16) if a.dtype == jnp.float32 else a, x)
 
 
-def local(queries, keys, values, chosen):
+def split_heads(queries, keys, values, chosen):
     scale = HD ** (-0.5)
     blk_count = lax.axis_size("blk")
     rank = lax.axis_index("blk")
@@ -110,8 +330,15 @@
     return returned.reshape(tok, kv_heads * GROUP * HD)
 
 
+def local(queries, keys, values, chosen):
+    count = lax.axis_size(AXES)
+    if queries.shape[0] == BS and BS % (16 * count) == 0:
+        return resident(queries, keys, values, chosen)
+    return split_heads(queries, keys, values, chosen)
+
+
 def solution(mesh):
-    placed = (P(("blk", "uly"), None), P(("blk", "uly"), None), P(("blk", "uly"), None), P())
+    placed = (P(AXES, None), P(AXES, None), P(AXES, None), P())
     return jax.shard_map(
-        local, mesh=mesh, in_specs=placed, out_specs=P(("blk", "uly"), None), check_vma=False
-    )
+        local, mesh=mesh, in_specs=placed, out_specs=P(AXES, None), check_vma=False
+    )

time: 361 us -> 70.1 us (0.19)
  local copies, waits for them, and re-layouts: 88 us -> 4.51 us
  matrix products: 68.9 us -> 0 us
  other arithmetic: 45.2 us -> 0.23 us
  loops' own time: 41.1 us -> 0 us
  blocking collectives: 41 us -> 0 us
  waiting for transfers between devices: 57.8 us -> 33.1 us
  Pallas kernels: 0 us -> 20.9 us
  starting transfers between devices: 14.9 us -> 10.9 us
    dot_general x64 -> x0, matrix products: 68.9 us -> none  [the longest x16 23.2 us: finish(): lax.dot_general(query_rows, routed_kv[:, :HD], contract, preferred_elemen...]
    another operation x1 -> x0, loops' own time: 41.1 us -> none  [local(): result = lax.map(with_late, items)]
    all_to_all x2 -> x0, blocking collectives: 41 us -> none  [the longest x1 29 us: local(): lax.all_to_all(as_sent(gathered), 'uly', split_axis=0, concat_axis=1, til...]
    all_to_all x3 -> x2, waiting for transfers between devices: 57.8 us -> 33.1 us  [the longest x1 26 us: resident(): routed = lax.all_to_all(request, AXES, 0, 0, tiled=True)]
    dynamic_slice x68 -> x0, local copies, waits for them, and re-layouts: 24 us -> none  [the longest x32 14.2 us: own_part(): lax.dynamic_index_in_dim(own_rows, item // GROUP, 0, keepdims=False)]
    pallas_call x0 -> x3, Pallas kernels: none -> 20.9 us  [the longest x1 12.9 us: attend_routed(): pl.pallas_call(routed_kernel, grid_spec=pltpu.PrefetchScalarGridSpec(num_...]
    gather x17 -> x1, other arithmetic: 19.6 us -> 0.01 us  [resident(): request = table[wanted].reshape(count, kv_heads * 2, BS // count, 2 * HD)]
    squeeze x16 -> x0, local copies, waits for them, and re-layouts: 17.3 us -> none  [finish(): routed_kv = lax.dynamic_index_in_dim(picked, index, 0, keepdims=False)]
  transfers between devices with their start and end apart: 3 -> 2, of which waited for: 3 -> 2; matrix products, arithmetic and copies ran while one was open for 2% -> 1% of each run, Pallas kernels for 0% -> 9%
where the time goes in v2:
time: 70.1 us; the launch traced here: 69.7 us
  waiting for transfers between devices  33.1 us (47%)
  Pallas kernels  20.9 us (30%)
  starting transfers between devices  10.9 us (16%)
  local copies, waits for them, and re-layouts  4.51 us (6%)
    all_to_all x1, waiting for transfers between devices, resident(): routed = lax.all_to_all(request, AXES, 0, 0, tiled=True)  26 us
    pallas_call x1, Pallas kernels, attend_routed(): pl.pallas_call(routed_kernel, grid_spec=pltpu.PrefetchScalarGridSpec(num_...  12.9 us
    all_to_all x1, starting transfers between devices, resident(): table = lax.all_to_all(pack(keys, values, count), AXES, 0, 0, tiled=True)  7.3 us
    all_to_all x1, waiting for transfers between devices, resident(): table = lax.all_to_all(pack(keys, values, count), AXES, 0, 0, tiled=True)  7.08 us
    pallas_call x1, Pallas kernels, attend_own(): pl.pallas_call(own_kernel, grid=(heads // STEP,), in_specs=[pl.BlockSpec(...  6.02 us
    all_to_all x1, starting transfers between devices, resident(): routed = lax.all_to_all(request, AXES, 0, 0, tiled=True)  3.62 us
    unnamed x14, local copies, waits for them, and re-layouts  2.65 us
    pallas_call x1, Pallas kernels, pack(): pl.pallas_call(pack_kernel, out_shape=jax.ShapeDtypeStruct(shape, keys.dt...  1.98 us
  transfers between devices with their start and end apart: 2, of which 2 were waited for; matrix products, arithmetic and copies ran while one was open for 1% of the time, Pallas kernels for 9%

profile of v2, /device:TPU:0, one launch (start us, length us, event | category | flops | bytes accessed | tf_op | source)
XLA Modules:
  0.0 69.7 jit_solution(1363059107710463106)
XLA Ops:
  0.0 0.0 copy-start
  0.0 0.0 copy-start.6
  0.0 2.0 %pack.1 = bf16[32,2,16,256]{3,2,1,0:T(8,128)(2,1)} custom-call(bf16[512,256]{1,0:T(8,128)(2,1)} %first_key_ref.1, bf16[512,256]{1,0:T(8,128)(2,1)} %v_ref.3), custom_call_target="tpu_custom_call" | custom-call | tf_op jit(solution)/shard_map/pack/pallas_call | solution.py:211
  2.0 7.3 %all-to-all-start = ((bf16[32,2,16,256]{3,2,1,0:T(8,128)(2,1)}), bf16[32,2,16,256]{3,2,1,0:T(8,128)(2,1)S(1)}, u32[]{:S(2)}, u32[]{:S(2)}) async-start(bf16[32,2,16,256]{3,2,1,0:T(8,128)(2,1)} %pack.1), calls=%async_computation | async-start | bytes 1048576 | tf_op jit(solution)/shard_map/all_to_all | solution.py:222
  9.3 0.0 copy-done.6
  9.3 0.1 copy.6
  9.4 0.1 reshape.13
  9.6 0.0 copy-done.1
  9.6 0.0 copy-done
  9.6 0.0 copy-start.2
  9.6 1.6 %copy-done.2 = bf16[512,2048]{1,0:T(8,128)(2,1)S(1)} copy-done((bf16[512,2048]{1,0:T(8,128)(2,1)S(1)}, bf16[512,2048]{1,0:T(8,128)(2,1)}, u32[]{:S(2)}) %copy-start.2) | copy-done | bytes 2097176
  11.2 6.0 %attend_own.1 = (f32[512,2048]{1,0:T(8,128)}, f32[512,256]{1,0:T(8,128)S(1)}) custom-call(bf16[512,2048]{1,0:T(8,128)(2,1)S(1)} %copy-done.2, bf16[512,256]{1,0:T(8,128)(2,1)S(1)} %copy-done.1, bf16[512,256]{1,0:T(8,128)(2,1)S(1)} %copy-done), custom_call_target="tpu_custom_call" | custom-call | flops 1610612736 | bytes 6291456 | tf_op jit(solution)/shard_map/attend_own/pallas_call | solution.py:80
  17.2 0.0 copy-start.4
  17.2 7.1 %all-to-all-done = bf16[32,2,16,256]{3,2,1,0:T(8,128)(2,1)S(1)} async-done(((bf16[32,2,16,256]{3,2,1,0:T(8,128)(2,1)}), bf16[32,2,16,256]{3,2,1,0:T(8,128)(2,1)S(1)}, u32[]{:S(2)}, u32[]{:S(2)}) %all-to-all-start) | async-done | bytes 524320 | tf_op jit(solution)/shard_map/all_to_all | solution.py:222
  24.3 0.0 copy-start.3
  24.3 1.6 %gather_fusion = bf16[128,16,256]{2,1,0:T(8,128)(2,1)} fusion(bf16[64,16,256]{2,1,0:T(8,128)(2,1)S(1)} %bitcast.2, s32[1024]{0:T(1024)S(1)} %pad_clamp_fusion), kind=kCustom, calls=%fused_computation | custom fusion | bytes 2097664 | tf_op jit(solution)/shard_map/gather | solution.py:226
  25.9 0.0 copy-done.4
  25.9 3.6 %all-to-all-start.1 = ((bf16[32,4,16,256]{3,2,1,0:T(8,128)(2,1)}), bf16[32,4,16,256]{3,2,1,0:T(8,128)(2,1)S(1)}, u32[]{:S(2)}, u32[]{:S(2)}) async-start(bf16[32,4,16,256]{3,2,1,0:T(8,128)(2,1)} %bitcast.3), calls=%async_computation.1 | async-start | bytes 2097152 | tf_op jit(solution)/shard_map/all_to_all | solution.py:227
  29.5 0.2 fusion.usable
  29.8 26.0 %all-to-all-done.1.routed_ref = bf16[32,4,16,256]{3,2,1,0:T(8,128)(2,1)S(1)} async-done(((bf16[32,4,16,256]{3,2,1,0:T(8,128)(2,1)}), bf16[32,4,16,256]{3,2,1,0:T(8,128)(2,1)S(1)}, u32[]{:S(2)}, u32[]{:S(2)}) %all-to-all-start.1) | async-done | bytes 1048608 | tf_op jit(solution)/shard_map/all_to_all | solution.py:227
  55.8 0.0 copy-done.3
  55.8 0.0 copy-start.5
  55.8 1.0 %copy-done.5 = f32[512,256]{1,0:T(8,128)S(1)} copy-done((f32[512,256]{1,0:T(8,128)S(1)}, f32[512,256]{1,0:T(8,128)}, u32[]{:S(2)}) %copy-start.5) | copy-done | bytes 524312
  56.8 12.9 %attend_routed.1 = bf16[512,2048]{1,0:T(8,128)(2,1)} custom-call(s32[2,2]{1,0:T(2,128)S(1)} %fusion.usable, bf16[512,2048]{1,0:T(8,128)(2,1)S(1)} %copy-done.3, bf16[512,256]{1,0:T(8,128)(2,1)S(1)} %copy-done.1, f32[512,2048]{1,0:T(8,128)} %get-tuple-element.9.sum_ref, f32[512,256]{1,0:T(8,128)S(1)} %copy-done.5, ...), custom_call_target="tpu_custom_call" | custom-call | flops 4294967296 | bytes 9437184 | tf_op jit(solution)/shard_map/attend_routed/pallas_call | solution.py:176
  (4 shorter events, 0.0 us)
Async XLA Ops:
  0.0 9.6 %copy-start.1 = (bf16[512,256]{1,0:T(8,128)(2,1)S(1)}, bf16[512,256]{1,0:T(8,128)(2,1)}, u32[]{:S(2)}) copy-start(bf16[512,256]{1,0:T(8,128)(2,1)} %first_key_ref.1) | copy-start | bytes 786436
  0.0 9.6 %copy-start = (bf16[512,256]{1,0:T(8,128)(2,1)S(1)}, bf16[512,256]{1,0:T(8,128)(2,1)}, u32[]{:S(2)}) copy-start(bf16[512,256]{1,0:T(8,128)(2,1)} %v_ref.3) | copy-start | bytes 786436
  0.0 9.3 %copy-start.6 = (s32[32,2,2]{0,2,1:T(2,128)S(1)}, s32[32,2,2]{0,2,1:T(2,128)}, u32[]{:S(2)}) copy-start(s32[32,2,2]{0,2,1:T(2,128)} %param.7) | copy-start | bytes 1540
  2.0 22.3 %all-to-all-start = ((bf16[32,2,16,256]{3,2,1,0:T(8,128)(2,1)}), bf16[32,2,16,256]{3,2,1,0:T(8,128)(2,1)S(1)}, u32[]{:S(2)}, u32[]{:S(2)}) async-start(bf16[32,2,16,256]{3,2,1,0:T(8,128)(2,1)} %pack.1), calls=%async_computation | async-start | bytes 1048576 | tf_op jit(solution)/shard_map/all_to_all | solution.py:222
  9.6 1.6 %copy-start.2 = (bf16[512,2048]{1,0:T(8,128)(2,1)S(1)}, bf16[512,2048]{1,0:T(8,128)(2,1)}, u32[]{:S(2)}) copy-start(bf16[512,2048]{1,0:T(8,128)(2,1)} %q_ref.3) | copy-start | bytes 6291460
  17.2 8.7 %copy-start.4 = (f32[512,256]{1,0:T(8,128)}, f32[512,256]{1,0:T(8,128)S(1)}, u32[]{:S(2)}) copy-start(f32[512,256]{1,0:T(8,128)S(1)} %get-tuple-element.11.stat_ref) | copy-start | bytes 1572868
  24.3 31.5 %copy-start.3 = (bf16[512,2048]{1,0:T(8,128)(2,1)S(1)}, bf16[512,2048]{1,0:T(8,128)(2,1)}, u32[]{:S(2)}) copy-start(bf16[512,2048]{1,0:T(8,128)(2,1)} %q_ref.3) | copy-start | bytes 6291460
  25.9 29.9 %all-to-all-start.1 = ((bf16[32,4,16,256]{3,2,1,0:T(8,128)(2,1)}), bf16[32,4,16,256]{3,2,1,0:T(8,128)(2,1)S(1)}, u32[]{:S(2)}, u32[]{:S(2)}) async-start(bf16[32,4,16,256]{3,2,1,0:T(8,128)(2,1)} %bitcast.3), calls=%async_computation.1 | async-start | bytes 2097152 | tf_op jit(solution)/shard_map/all_to_all | solution.py:227
  55.8 1.0 %copy-start.5 = (f32[512,256]{1,0:T(8,128)S(1)}, f32[512,256]{1,0:T(8,128)}, u32[]{:S(2)}) copy-start(f32[512,256]{1,0:T(8,128)} %copy-done.4) | copy-start | bytes 1572868

commit v3 on v2

--- a/solution.py
+++ b/solution.py
@@ -18,20 +18,20 @@
 EXPONENT = HD ** (-0.5) * math.log2(math.e)
 
 
-def scores_of(rows, key_rows):
+def scores_of(key_rows, rows):
     return lax.dot_general(
-        rows, key_rows, (((1,), (1,)), ((), ())), preferred_element_type=jnp.float32
-    )
-
-
-def weighted(scores, top, values):
+        key_rows, rows, (((1,), (1,)), ((), ())), preferred_element_type=jnp.float32
+    )
+
+
+def weighted(values, scores, top):
     weights = jnp.exp2(scores * EXPONENT - top).astype(jnp.bfloat16)
-    return jnp.dot(weights, values, preferred_element_type=jnp.float32)
-
-
-def lane_max(scores):
-    parts = [scores[:, i : i + HD] for i in range(0, scores.shape[1], HD)]
-    return functools.reduce(jnp.maximum, parts)
+    both = jnp.dot(values, weights, preferred_element_type=jnp.float32)
+    return both[:HD], both[HD : HD + 1]
+
+
+def over_ones(values, ones):
+    return jnp.concatenate([values.T, ones], axis=0)
 
 
 def staggered(items, first, second):
@@ -42,37 +42,29 @@
         held = ahead
 
 
-def with_ones(values):
-    return jnp.concatenate([values, jnp.ones_like(values)], axis=1)
-
-
 def own_kernel(q_ref, k_ref, v_ref, sum_ref, stat_ref):
     keys = k_ref[...]
-    values = with_ones(v_ref[...])
+    values = over_ones(v_ref[...], jnp.ones((16, BS), jnp.bfloat16))
     shape = (TILE, TILE)
-    causal = lax.broadcasted_iota(jnp.int32, shape, 1) <= lax.broadcasted_iota(jnp.int32, shape, 0)
-    lane = lax.broadcasted_iota(jnp.int32, (TILE, HD), 1)
-    stats = {}
+    causal = lax.broadcasted_iota(jnp.int32, shape, 0) <= lax.broadcasted_iota(jnp.int32, shape, 1)
 
     def first(item):
         h, start = item
         rows = q_ref[start : start + TILE, h * HD : (h + 1) * HD]
-        return scores_of(rows, keys[: start + TILE])
+        return scores_of(keys[: start + TILE], rows)
 
     def second(item, scores):
         h, start = item
-        diagonal = jnp.where(causal, scores[:, start:], -jnp.inf)
-        scores = jnp.concatenate([scores[:, :start], diagonal], axis=1) if start else diagonal
-        top = jnp.max(lane_max(scores), axis=1, keepdims=True) * EXPONENT
-        both = weighted(scores, top, values[: start + TILE])
-        sum_ref[start : start + TILE, h * HD : (h + 1) * HD] = both[:, :HD]
-        stat = stats.get(start, jnp.zeros((TILE, HD), jnp.float32))
-        stat = jnp.where(lane == h, top, stat)
-        stats[start] = jnp.where(lane == STEP + h, both[:, HD:], stat)
+        here = slice(start, start + TILE)
+        diagonal = jnp.where(causal, scores[start:], -jnp.inf)
+        scores = jnp.concatenate([scores[:start], diagonal], axis=0) if start else diagonal
+        top = jnp.max(scores, axis=0, keepdims=True) * EXPONENT
+        summed, total = weighted(values[:, : start + TILE], scores, top)
+        sum_ref[h * HD : (h + 1) * HD, here] = summed
+        stat_ref[h : h + 1, here] = top
+        stat_ref[STEP + h : STEP + h + 1, here] = total
 
     staggered([(h, t) for h in range(STEP) for t in range(0, BS, TILE)], first, second)
-    for start, stat in stats.items():
-        stat_ref[start : start + TILE, :] = stat
 
 
 def attend_own(queries, keys, values):
@@ -86,12 +78,12 @@
             pl.BlockSpec((BS, HD), lambda i: (0, i * STEP // GROUP)),
         ],
         out_specs=[
-            pl.BlockSpec((BS, STEP * HD), lambda i: (0, i)),
-            pl.BlockSpec((BS, HD), lambda i: (0, i)),
+            pl.BlockSpec((STEP * HD, BS), lambda i: (i, 0)),
+            pl.BlockSpec((2 * STEP, BS), lambda i: (i, 0)),
         ],
         out_shape=[
-            jax.ShapeDtypeStruct(queries.shape, jnp.float32),
-            jax.ShapeDtypeStruct((BS, heads // STEP * HD), jnp.float32),
+            jax.ShapeDtypeStruct((heads * HD, BS), jnp.float32),
+            jax.ShapeDtypeStruct((heads * 2, BS), jnp.float32),
         ],
         compiler_params=pltpu.CompilerParams(vmem_limit_bytes=48 * 2**20),
         cost_estimate=pl.CostEstimate(
@@ -107,7 +99,6 @@
     kv_head = pl.program_id(0) * STEP // GROUP
     use = [usable[kv_head, s] != 0 for s in range(2)]
     none = jnp.zeros((), jnp.bfloat16)
-    ones = jnp.ones((BS, HD), jnp.bfloat16)
     slots = range(2)
     keys = jnp.concatenate(
         [
@@ -117,75 +108,63 @@
         axis=0,
     )
     values = jnp.concatenate(
-        [
-            jnp.concatenate(
-                [
-                    jnp.where(use[s], routed_ref[:, s, :, HD:].reshape(BS, HD), none),
-                    jnp.where(use[s], ones, none),
-                ],
-                axis=1,
-            )
-            for s in slots
-        ],
-        axis=0,
-    )
+        [jnp.where(use[s], routed_ref[:, s, :, HD:].reshape(BS, HD), none) for s in slots], axis=0
+    )
+    ones = jnp.ones((16, BS), jnp.bfloat16)
+    ones = jnp.concatenate([jnp.where(use[s], ones, none) for s in slots], axis=1)
+    values = over_ones(values, ones)
     seen = []
 
     def first(item):
         h, start = item
-        return scores_of(q_ref[start : start + TILE, h * HD : (h + 1) * HD], keys)
+        return scores_of(keys, q_ref[start : start + TILE, h * HD : (h + 1) * HD])
 
     def second(item, scores):
         h, start = item
-        here = slice(start, start + TILE), slice(h * HD, (h + 1) * HD)
-        own_top = stat_ref[start : start + TILE, h : h + 1]
-        own_total = stat_ref[start : start + TILE, STEP + h : STEP + h + 1]
-        both = weighted(scores, own_top, values)
-        total = both[:, HD:] + own_total
+        rows, part = slice(start, start + TILE), slice(h * HD, (h + 1) * HD)
+        summed, total = weighted(values, scores, stat_ref[h : h + 1, rows])
+        total = total + stat_ref[STEP + h : STEP + h + 1, rows]
         seen.append(total)
-        out_ref[here] = ((both[:, :HD] + sum_ref[here]) / total).astype(out_ref.dtype)
+        summed = (summed + sum_ref[part, rows]) / total
+        out_ref[rows, part] = summed.astype(out_ref.dtype).T
 
     staggered([(h, t) for h in range(STEP) for t in range(0, BS, TILE)], first, second)
     in_range = functools.reduce(jnp.logical_and, [total < ROOM for total in seen])
 
     @pl.when(jnp.logical_not(jnp.all(in_range)))
     def _():
-        lane = lax.broadcasted_iota(jnp.int32, (TILE, HD), 1)
-
-        @pl.loop(0, STEP * (BS // TILE))
-        def _(item):
-            h = item // (BS // TILE)
-            rows = pl.ds(pl.multiple_of(item % (BS // TILE) * TILE, TILE), TILE)
-            here = rows, pl.ds(pl.multiple_of(h * HD, HD), HD)
-            stat = stat_ref[rows, :]
-            own_top = jnp.sum(jnp.where(lane == h, stat, 0.0), axis=1, keepdims=True)
-            own_total = jnp.sum(jnp.where(lane == STEP + h, stat, 0.0), axis=1, keepdims=True)
-            scores = scores_of(q_ref[here], keys)
-            top = jnp.max(lane_max(scores), axis=1, keepdims=True) * EXPONENT
-            top = jnp.maximum(top, own_top)
-            scale = jnp.exp2(own_top - top)
-            both = weighted(scores, top, values)
-            total = both[:, HD:] + own_total * scale
-            out_ref[here] = ((both[:, :HD] + sum_ref[here] * scale) / total).astype(out_ref.dtype)
+        @pl.loop(0, STEP)
+        def _(h):
+            part = pl.ds(pl.multiple_of(h * HD, HD), HD)
+            for start in range(0, BS, TILE):
+                rows = slice(start, start + TILE)
+                own_top = stat_ref[pl.ds(h, 1), rows]
+                own_total = stat_ref[pl.ds(STEP + h, 1), rows]
+                scores = scores_of(keys, q_ref[rows, part])
+                top = jnp.max(scores, axis=0, keepdims=True) * EXPONENT
+                top = jnp.maximum(top, own_top)
+                scale = jnp.exp2(own_top - top)
+                summed, total = weighted(values, scores, top)
+                summed = (summed + sum_ref[part, rows] * scale) / (total + own_total * scale)
+                out_ref[rows, part] = summed.astype(out_ref.dtype).T
 
 
 def attend_routed(usable, queries, keys, own_sum, own_stat, routed):
     shares, _, rows, _ = routed.shape
     heads = queries.shape[1] // HD
-    here = lambda i, u: (0, i)
     return pl.pallas_call(
         routed_kernel,
         grid_spec=pltpu.PrefetchScalarGridSpec(
             num_scalar_prefetch=1,
             grid=(heads // STEP,),
             in_specs=[
-                pl.BlockSpec((BS, STEP * HD), here),
+                pl.BlockSpec((BS, STEP * HD), lambda i, u: (0, i)),
                 pl.BlockSpec((16, HD), lambda i, u: (0, i * STEP // GROUP)),
-                pl.BlockSpec((BS, STEP * HD), here),
-                pl.BlockSpec((BS, HD), here),
+                pl.BlockSpec((STEP * HD, BS), lambda i, u: (i, 0)),
+                pl.BlockSpec((2 * STEP, BS), lambda i, u: (i, 0)),
                 pl.BlockSpec((shares, 2, rows, 2 * HD), lambda i, u: (0, i * STEP // GROUP, 0, 0)),
             ],
-            out_specs=pl.BlockSpec((BS, STEP * HD), here),
+            out_specs=pl.BlockSpec((BS, STEP * HD), lambda i, u: (0, i)),
         ),
         out_shape=jax.ShapeDtypeStruct(queries.shape, queries.dtype),
         compiler_params=pltpu.CompilerParams(vmem_limit_bytes=48 * 2**20),

time: 70.1 us -> 67.4 us (0.961)
  local copies, waits for them, and re-layouts: 4.51 us -> 3.46 us
  waiting for transfers between devices: 33.1 us -> 32.2 us
    pallas_call x1, Pallas kernels: 12.9 us -> 11.3 us  [attend_routed(): pl.pallas_call(routed_kernel, grid_spec=pltpu.PrefetchScalarGridSpec(num_...]
    unnamed x14 -> x10, local copies, waits for them, and re-layouts: 2.65 us -> 1.6 us
    pallas_call x1, Pallas kernels: 6.02 us -> 6.94 us  [attend_own(): pl.pallas_call(own_kernel, grid=(heads // STEP,), in_specs=[pl.BlockSpec(...]
    all_to_all x1, waiting for transfers between devices: 7.08 us -> 6.16 us  [resident(): table = lax.all_to_all(pack(keys, values, count), AXES, 0, 0, tiled=True)]
  transfers between devices with their start and end apart: 2 -> 2, of which waited for: 2 -> 2; matrix products, arithmetic and copies ran while one was open for 1% -> 1% of each run, Pallas kernels for 9% -> 10%
where the time goes in v3:
time: 67.4 us; the launch traced here: 67.1 us
  waiting for transfers between devices  32.2 us (48%)
  Pallas kernels  20.2 us (30%)
  starting transfers between devices  10.9 us (16%)
  local copies, waits for them, and re-layouts  3.46 us (5%)
    all_to_all x1, waiting for transfers between devices, resident(): routed = lax.all_to_all(request, AXES, 0, 0, tiled=True)  26 us
    pallas_call x1, Pallas kernels, attend_routed(): pl.pallas_call(routed_kernel, grid_spec=pltpu.PrefetchScalarGridSpec(num_...  11.3 us
    all_to_all x1, starting transfers between devices, resident(): table = lax.all_to_all(pack(keys, values, count), AXES, 0, 0, tiled=True)  7.3 us
    pallas_call x1, Pallas kernels, attend_own(): pl.pallas_call(own_kernel, grid=(heads // STEP,), in_specs=[pl.BlockSpec(...  6.94 us
    all_to_all x1, waiting for transfers between devices, resident(): table = lax.all_to_all(pack(keys, values, count), AXES, 0, 0, tiled=True)  6.16 us
    all_to_all x1, starting transfers between devices, resident(): routed = lax.all_to_all(request, AXES, 0, 0, tiled=True)  3.62 us
    pallas_call x1, Pallas kernels, pack(): pl.pallas_call(pack_kernel, out_shape=jax.ShapeDtypeStruct(shape, keys.dt...  1.98 us
    gather x1, local copies, waits for them, and re-layouts, resident(): request = table[wanted].reshape(count, kv_heads * 2, BS // count, 2 * HD)  1.61 us
  transfers between devices with their start and end apart: 2, of which 2 were waited for; matrix products, arithmetic and copies ran while one was open for 1% of the time, Pallas kernels for 10%

profile of v3, /device:TPU:0, one launch (start us, length us, event | category | flops | bytes accessed | tf_op | source)
XLA Modules:
  0.0 67.1 jit_solution(10630871604957651366)
XLA Ops:
  0.0 0.0 copy-start.1
  0.0 0.0 copy-start
  0.0 0.0 copy-start.4
  0.0 2.0 %pack.1 = bf16[32,2,16,256]{3,2,1,0:T(8,128)(2,1)} custom-call(bf16[512,256]{1,0:T(8,128)(2,1)} %first_key_ref.1, bf16[512,256]{1,0:T(8,128)(2,1)} %v_ref.3), custom_call_target="tpu_custom_call" | custom-call | tf_op jit(solution)/shard_map/pack/pallas_call | solution.py:190
  2.0 7.3 %all-to-all-start = ((bf16[32,2,16,256]{3,2,1,0:T(8,128)(2,1)}), bf16[32,2,16,256]{3,2,1,0:T(8,128)(2,1)S(1)}, u32[]{:S(2)}, u32[]{:S(2)}) async-start(bf16[32,2,16,256]{3,2,1,0:T(8,128)(2,1)} %pack.1), calls=%async_computation | async-start | bytes 1048576 | tf_op jit(solution)/shard_map/all_to_all | solution.py:201
  9.3 0.0 copy-done.4
  9.3 0.1 copy.6
  9.4 0.1 reshape.13
  9.6 0.0 copy-done.1
  9.6 0.0 copy-done
  9.6 0.0 copy-start.2
  9.6 1.6 %copy-done.2 = bf16[512,2048]{1,0:T(8,128)(2,1)S(1)} copy-done((bf16[512,2048]{1,0:T(8,128)(2,1)S(1)}, bf16[512,2048]{1,0:T(8,128)(2,1)}, u32[]{:S(2)}) %copy-start.2) | copy-done | bytes 2097176
  11.2 6.9 %attend_own.1 = (f32[2048,512]{1,0:T(8,128)}, f32[32,512]{1,0:T(8,128)S(1)}) custom-call(bf16[512,2048]{1,0:T(8,128)(2,1)S(1)} %copy-done.2, bf16[512,256]{1,0:T(8,128)(2,1)S(1)} %copy-done.1, bf16[512,256]{1,0:T(8,128)(2,1)S(1)} %copy-done), custom_call_target="tpu_custom_call" | custom-call | flops 1610612736 | bytes 6291456 | tf_op jit(solution)/shard_map/attend_own/pallas_call | solution.py:72
  18.1 6.2 %all-to-all-done = bf16[32,2,16,256]{3,2,1,0:T(8,128)(2,1)S(1)} async-done(((bf16[32,2,16,256]{3,2,1,0:T(8,128)(2,1)}), bf16[32,2,16,256]{3,2,1,0:T(8,128)(2,1)S(1)}, u32[]{:S(2)}, u32[]{:S(2)}) %all-to-all-start) | async-done | bytes 524320 | tf_op jit(solution)/shard_map/all_to_all | solution.py:201
  24.3 0.0 copy-start.3
  24.3 1.6 %gather_fusion = bf16[128,16,256]{2,1,0:T(8,128)(2,1)} fusion(bf16[64,16,256]{2,1,0:T(8,128)(2,1)S(1)} %bitcast.2, s32[1024]{0:T(1024)S(1)} %pad_clamp_fusion), kind=kCustom, calls=%fused_computation | custom fusion | bytes 2097664 | tf_op jit(solution)/shard_map/gather | solution.py:205
  25.9 3.6 %all-to-all-start.1 = ((bf16[32,4,16,256]{3,2,1,0:T(8,128)(2,1)}), bf16[32,4,16,256]{3,2,1,0:T(8,128)(2,1)S(1)}, u32[]{:S(2)}, u32[]{:S(2)}) async-start(bf16[32,4,16,256]{3,2,1,0:T(8,128)(2,1)} %bitcast.3), calls=%async_computation.1 | async-start | bytes 2097152 | tf_op jit(solution)/shard_map/all_to_all | solution.py:206
  29.5 0.2 fusion.usable
  29.8 26.0 %all-to-all-done.1.routed_ref = bf16[32,4,16,256]{3,2,1,0:T(8,128)(2,1)S(1)} async-done(((bf16[32,4,16,256]{3,2,1,0:T(8,128)(2,1)}), bf16[32,4,16,256]{3,2,1,0:T(8,128)(2,1)S(1)}, u32[]{:S(2)}, u32[]{:S(2)}) %all-to-all-start.1) | async-done | bytes 1048608 | tf_op jit(solution)/shard_map/all_to_all | solution.py:206
  55.8 0.0 copy-done.3
  55.8 11.3 %attend_routed.1 = bf16[512,2048]{1,0:T(8,128)(2,1)} custom-call(s32[2,2]{1,0:T(2,128)S(1)} %fusion.usable, bf16[512,2048]{1,0:T(8,128)(2,1)S(1)} %copy-done.3, bf16[512,256]{1,0:T(8,128)(2,1)S(1)} %copy-done.1, f32[2048,512]{1,0:T(8,128)} %get-tuple-element.9.sum_ref, f32[32,512]{1,0:T(8,128)S(1)} %get-tuple-element.11.stat_ref, ...), custom_call_target="tpu_custom_call" | custom-call | flops 4294967296 | bytes 9437184 | tf_op jit(solution)/shard_map/attend_routed/pallas_call | solution.py:155
  (3 shorter events, 0.0 us)
Async XLA Ops:
  0.0 9.6 %copy-start.1 = (bf16[512,256]{1,0:T(8,128)(2,1)S(1)}, bf16[512,256]{1,0:T(8,128)(2,1)}, u32[]{:S(2)}) copy-start(bf16[512,256]{1,0:T(8,128)(2,1)} %first_key_ref.1) | copy-start | bytes 786436
  0.0 9.6 %copy-start = (bf16[512,256]{1,0:T(8,128)(2,1)S(1)}, bf16[512,256]{1,0:T(8,128)(2,1)}, u32[]{:S(2)}) copy-start(bf16[512,256]{1,0:T(8,128)(2,1)} %v_ref.3) | copy-start | bytes 786436
  0.0 9.3 %copy-start.4 = (s32[32,2,2]{0,2,1:T(2,128)S(1)}, s32[32,2,2]{0,2,1:T(2,128)}, u32[]{:S(2)}) copy-start(s32[32,2,2]{0,2,1:T(2,128)} %param.7) | copy-start | bytes 1540
  2.0 22.3 %all-to-all-start = ((bf16[32,2,16,256]{3,2,1,0:T(8,128)(2,1)}), bf16[32,2,16,256]{3,2,1,0:T(8,128)(2,1)S(1)}, u32[]{:S(2)}, u32[]{:S(2)}) async-start(bf16[32,2,16,256]{3,2,1,0:T(8,128)(2,1)} %pack.1), calls=%async_computation | async-start | bytes 1048576 | tf_op jit(solution)/shard_map/all_to_all | solution.py:201
  9.6 1.6 %copy-start.2 = (bf16[512,2048]{1,0:T(8,128)(2,1)S(1)}, bf16[512,2048]{1,0:T(8,128)(2,1)}, u32[]{:S(2)}) copy-start(bf16[512,2048]{1,0:T(8,128)(2,1)} %q_ref.3) | copy-start | bytes 6291460
  24.3 31.5 %copy-start.3 = (bf16[512,2048]{1,0:T(8,128)(2,1)S(1)}, bf16[512,2048]{1,0:T(8,128)(2,1)}, u32[]{:S(2)}) copy-start(bf16[512,2048]{1,0:T(8,128)(2,1)} %q_ref.3) | copy-start | bytes 6291460
  25.9 29.9 %all-to-all-start.1 = ((bf16[32,4,16,256]{3,2,1,0:T(8,128)(2,1)}), bf16[32,4,16,256]{3,2,1,0:T(8,128)(2,1)S(1)}, u32[]{:S(2)}, u32[]{:S(2)}) async-start(bf16[32,4,16,256]{3,2,1,0:T(8,128)(2,1)} %bitcast.3), calls=%async_computation.1 | async-start | bytes 2097152 | tf_op jit(solution)/shard_map/all_to_all | solution.py:206

commit v4 on v3

--- a/solution.py
+++ b/solution.py
@@ -13,6 +13,9 @@
 GROUP = 8
 AXES = ("blk", "uly")
 TILE = 256
+CHUNK = 256
+EARLY = 4
+CUT = 12
 STEP = GROUP
 ROOM = 2.0**100
 EXPONENT = HD ** (-0.5) * math.log2(math.e)
@@ -95,86 +98,129 @@
     )(queries, keys, values)
 
 
-def routed_kernel(usable, q_ref, first_key_ref, sum_ref, stat_ref, routed_ref, out_ref):
-    kv_head = pl.program_id(0) * STEP // GROUP
-    use = [usable[kv_head, s] != 0 for s in range(2)]
+def routed_kernel(
+    usable, q_ref, first_key_ref, sum_hbm, stat_ref, routed_ref, out_hbm, *scratch
+):
+    sum_ref, part_ref, total_ref, out_ref, sum_sem, out_sems = scratch
+    bring = pltpu.make_async_copy(sum_hbm, sum_ref, sum_sem)
+    bring.start()
+    kv_heads = first_key_ref.shape[1] // HD
+    heads = kv_heads * GROUP
     none = jnp.zeros((), jnp.bfloat16)
-    slots = range(2)
-    keys = jnp.concatenate(
-        [
-            jnp.where(use[s], routed_ref[:, s, :, :HD].reshape(BS, HD), first_key_ref[0:1, :])
-            for s in slots
-        ],
-        axis=0,
-    )
-    values = jnp.concatenate(
-        [jnp.where(use[s], routed_ref[:, s, :, HD:].reshape(BS, HD), none) for s in slots], axis=0
-    )
     ones = jnp.ones((16, BS), jnp.bfloat16)
-    ones = jnp.concatenate([jnp.where(use[s], ones, none) for s in slots], axis=1)
-    values = over_ones(values, ones)
+    keys, values = {}, {}
+    for g in range(kv_heads):
+        for s in range(2):
+            use = usable[g, s] != 0
+            some, first_key = routed_ref[:, 2 * g + s], first_key_ref[0:1, g * HD : (g + 1) * HD]
+            keys[g, s] = jnp.where(use, some[:, :, :HD].reshape(BS, HD), first_key)
+            values[g, s] = over_ones(
+                jnp.where(use, some[:, :, HD:].reshape(BS, HD), none), jnp.where(use, ones, none)
+            )
+    chunks = [(s, c) for s in range(2) for c in range(0, BS, CHUNK)]
     seen = []
 
+    def columns(head, count):
+        return pl.ds(head * HD, count * HD)
+
+    def take_out(n, head, count):
+        part = columns(head, count)
+        return pltpu.make_async_copy(out_ref.at[:, part], out_hbm.at[:, part], out_sems.at[n])
+
+    def stat_rows(h):
+        own = h // GROUP * 2 * GROUP + h % GROUP
+        return pl.ds(own, 1), pl.ds(GROUP + own, 1)
+
     def first(item):
         h, start = item
-        return scores_of(keys, q_ref[start : start + TILE, h * HD : (h + 1) * HD])
-
-    def second(item, scores):
-        h, start = item
-        rows, part = slice(start, start + TILE), slice(h * HD, (h + 1) * HD)
-        summed, total = weighted(values, scores, stat_ref[h : h + 1, rows])
-        total = total + stat_ref[STEP + h : STEP + h + 1, rows]
-        seen.append(total)
+        rows = q_ref[start : start + TILE, h * HD : (h + 1) * HD]
+        return [scores_of(keys[h // GROUP, s][c : c + CHUNK], rows) for s, c in chunks]
+
+    def finish(item, summed, total):
+        h, start = item
+        rows, part = slice(start, start + TILE), columns(h, 1)
         summed = (summed + sum_ref[part, rows]) / total
         out_ref[rows, part] = summed.astype(out_ref.dtype).T
 
-    staggered([(h, t) for h in range(STEP) for t in range(0, BS, TILE)], first, second)
+    def second(item, scores):
+        h, start = item
+        rows = slice(start, start + TILE)
+        own_top, own_total = stat_rows(h)
+        summed, total = 0.0, stat_ref[own_total, rows]
+        for (s, c), some in zip(chunks, scores):
+            more = weighted(values[h // GROUP, s][:, c : c + CHUNK], some, stat_ref[own_top, rows])
+            summed, total = summed + more[0], total + more[1]
+        seen.append(total)
+        if h >= EARLY:
+            finish(item, summed, total)
+            if h == CUT - 1 and start == BS - TILE:
+                take_out(0, 0, CUT).start()
+            return
+        part_ref[columns(h, 1), rows] = summed
+        total_ref[h : h + 1, rows] = total
+        if h == EARLY - 1 and start == BS - TILE:
+            bring.wait()
+            for h in range(EARLY):
+                for start in range(0, BS, TILE):
+                    rows = slice(start, start + TILE)
+                    finish((h, start), part_ref[columns(h, 1), rows], total_ref[h : h + 1, rows])
+
+    staggered([(h, t) for h in range(heads) for t in range(0, BS, TILE)], first, second)
+    take_out(1, CUT, heads - CUT).start()
+    take_out(0, 0, CUT).wait()
+    take_out(1, CUT, heads - CUT).wait()
     in_range = functools.reduce(jnp.logical_and, [total < ROOM for total in seen])
 
     @pl.when(jnp.logical_not(jnp.all(in_range)))
     def _():
-        @pl.loop(0, STEP)
-        def _(h):
-            part = pl.ds(pl.multiple_of(h * HD, HD), HD)
-            for start in range(0, BS, TILE):
-                rows = slice(start, start + TILE)
-                own_top = stat_ref[pl.ds(h, 1), rows]
-                own_total = stat_ref[pl.ds(STEP + h, 1), rows]
-                scores = scores_of(keys, q_ref[rows, part])
-                top = jnp.max(scores, axis=0, keepdims=True) * EXPONENT
-                top = jnp.maximum(top, own_top)
-                scale = jnp.exp2(own_top - top)
-                summed, total = weighted(values, scores, top)
-                summed = (summed + sum_ref[part, rows] * scale) / (total + own_total * scale)
-                out_ref[rows, part] = summed.astype(out_ref.dtype).T
+        for g in range(kv_heads):
+            all_keys = jnp.concatenate([keys[g, s] for s in range(2)], axis=0)
+            all_values = jnp.concatenate([values[g, s] for s in range(2)], axis=1)
+
+            @pl.loop(g * GROUP, (g + 1) * GROUP)
+            def _(h):
+                part = pl.ds(pl.multiple_of(h * HD, HD), HD)
+                for start in range(0, BS, TILE):
+                    rows = slice(start, start + TILE)
+                    own_top, own_total = [stat_ref[at, rows] for at in stat_rows(h)]
+                    scores = scores_of(all_keys, q_ref[rows, part])
+                    top = jnp.max(scores, axis=0, keepdims=True) * EXPONENT
+                    top = jnp.maximum(top, own_top)
+                    scale = jnp.exp2(own_top - top)
+                    summed, total = weighted(all_values, scores, top)
+                    summed = summed + sum_ref[part, rows] * scale
+                    total = total + own_total * scale
+                    out_ref[rows, part] = (summed / total).astype(out_ref.dtype).T
+
+        again = take_out(0, 0, heads)
+        again.start()
+        again.wait()
 
 
 def attend_routed(usable, queries, keys, own_sum, own_stat, routed):
-    shares, _, rows, _ = routed.shape
     heads = queries.shape[1] // HD
+    vmem, hbm = pl.BlockSpec(memory_space=pltpu.VMEM), pl.BlockSpec(memory_space=pltpu.HBM)
     return pl.pallas_call(
         routed_kernel,
-        grid_spec=pltpu.PrefetchScalarGridSpec(
-            num_scalar_prefetch=1,
-            grid=(heads // STEP,),
-            in_specs=[
-                pl.BlockSpec((BS, STEP * HD), lambda i, u: (0, i)),
-                pl.BlockSpec((16, HD), lambda i, u: (0, i * STEP // GROUP)),
-                pl.BlockSpec((STEP * HD, BS), lambda i, u: (i, 0)),
-                pl.BlockSpec((2 * STEP, BS), lambda i, u: (i, 0)),
-                pl.BlockSpec((shares, 2, rows, 2 * HD), lambda i, u: (0, i * STEP // GROUP, 0, 0)),
-            ],
-            out_specs=pl.BlockSpec((BS, STEP * HD), lambda i, u: (0, i)),
-        ),
+        in_specs=[pl.BlockSpec(memory_space=pltpu.SMEM), vmem, vmem, hbm, vmem, vmem],
+        out_specs=hbm,
         out_shape=jax.ShapeDtypeStruct(queries.shape, queries.dtype),
-        compiler_params=pltpu.CompilerParams(vmem_limit_bytes=48 * 2**20),
+        scratch_shapes=[
+            pltpu.VMEM(own_sum.shape, own_sum.dtype),
+            pltpu.VMEM((EARLY * HD, BS), jnp.float32),
+            pltpu.VMEM((8, BS), jnp.float32),
+            pltpu.VMEM(queries.shape, queries.dtype),
+            pltpu.SemaphoreType.DMA,
+            pltpu.SemaphoreType.DMA((2,)),
+        ],
+        compiler_params=pltpu.CompilerParams(vmem_limit_bytes=32 * 2**20),
         cost_estimate=pl.CostEstimate(
             flops=8 * BS * BS * HD * heads,
             bytes_accessed=8 * BS * heads * HD + 2 * routed.size,
             transcendentals=2 * BS * BS * heads,
         ),
         name="attend_routed",
-    )(usable, queries, keys, own_sum, own_stat, routed)
+    )(usable, queries, keys, pltpu.with_memory_space_constraint(own_sum, pltpu.HBM), own_stat, routed)
 
 
 def pack_kernel(k_ref, v_ref, out_ref):

time: 67.4 us -> 66.3 us (0.984)
  Pallas kernels: 20.2 us -> 18.9 us
    pallas_call x1, Pallas kernels: 11.3 us -> 9.98 us  [attend_routed(): pl.pallas_call(routed_kernel, in_specs=[pl.BlockSpec(memory_space=pltpu.S...]
  transfers between devices with their start and end apart: 2 -> 2, of which waited for: 2 -> 2; matrix products, arithmetic and copies ran while one was open for 1% -> 1% of each run, Pallas kernels for 10% -> 11%
where the time goes in v4:
time: 66.3 us; the launch traced here: 65.9 us
  waiting for transfers between devices  32.2 us (49%)
  Pallas kernels  18.9 us (29%)
  starting transfers between devices  10.9 us (16%)
  local copies, waits for them, and re-layouts  3.46 us (5%)
    all_to_all x1, waiting for transfers between devices, resident(): routed = lax.all_to_all(request, AXES, 0, 0, tiled=True)  26 us
    pallas_call x1, Pallas kernels, attend_routed(): pl.pallas_call(routed_kernel, in_specs=[pl.BlockSpec(memory_space=pltpu.S...  9.98 us
    all_to_all x1, starting transfers between devices, resident(): table = lax.all_to_all(pack(keys, values, count), AXES, 0, 0, tiled=True)  7.3 us
    pallas_call x1, Pallas kernels, attend_own(): pl.pallas_call(own_kernel, grid=(heads // STEP,), in_specs=[pl.BlockSpec(...  6.93 us
    all_to_all x1, waiting for transfers between devices, resident(): table = lax.all_to_all(pack(keys, values, count), AXES, 0, 0, tiled=True)  6.17 us
    all_to_all x1, starting transfers between devices, resident(): routed = lax.all_to_all(request, AXES, 0, 0, tiled=True)  3.62 us
    pallas_call x1, Pallas kernels, pack(): pl.pallas_call(pack_kernel, out_shape=jax.ShapeDtypeStruct(shape, keys.dt...  1.98 us
    gather x1, local copies, waits for them, and re-layouts, resident(): request = table[wanted].reshape(count, kv_heads * 2, BS // count, 2 * HD)  1.61 us
  transfers between devices with their start and end apart: 2, of which 2 were waited for; matrix products, arithmetic and copies ran while one was open for 1% of the time, Pallas kernels for 11%

profile of v4, /device:TPU:0, one launch (start us, length us, event | category | flops | bytes accessed | tf_op | source)
XLA Modules:
  0.0 65.9 jit_solution(2101223498677002504)
XLA Ops:
  0.0 0.0 copy-start.1
  0.0 0.0 copy-start
  0.0 0.0 copy-start.4
  0.0 2.0 %pack.1 = bf16[32,2,16,256]{3,2,1,0:T(8,128)(2,1)} custom-call(bf16[512,256]{1,0:T(8,128)(2,1)} %first_key_ref.1, bf16[512,256]{1,0:T(8,128)(2,1)} %v_ref.3), custom_call_target="tpu_custom_call" | custom-call | tf_op jit(solution)/shard_map/pack/pallas_call | solution.py:236
  2.0 7.3 %all-to-all-start = ((bf16[32,2,16,256]{3,2,1,0:T(8,128)(2,1)}), bf16[32,2,16,256]{3,2,1,0:T(8,128)(2,1)S(1)}, u32[]{:S(2)}, u32[]{:S(2)}) async-start(bf16[32,2,16,256]{3,2,1,0:T(8,128)(2,1)} %pack.1), calls=%async_computation | async-start | bytes 1048576 | tf_op jit(solution)/shard_map/all_to_all | solution.py:247
  9.3 0.0 copy-done.4
  9.3 0.1 copy.6
  9.4 0.1 reshape.13
  9.6 0.0 copy-done.1
  9.6 0.0 copy-done
  9.6 0.0 copy-start.2
  9.6 1.6 %copy-done.2 = bf16[512,2048]{1,0:T(8,128)(2,1)S(1)} copy-done((bf16[512,2048]{1,0:T(8,128)(2,1)S(1)}, bf16[512,2048]{1,0:T(8,128)(2,1)}, u32[]{:S(2)}) %copy-start.2) | copy-done | bytes 2097176
  11.2 6.9 %attend_own.1 = (f32[2048,512]{1,0:T(8,128)}, f32[32,512]{1,0:T(8,128)S(1)}) custom-call(bf16[512,2048]{1,0:T(8,128)(2,1)S(1)} %copy-done.2, bf16[512,256]{1,0:T(8,128)(2,1)S(1)} %copy-done.1, bf16[512,256]{1,0:T(8,128)(2,1)S(1)} %copy-done), custom_call_target="tpu_custom_call" | custom-call | flops 1610612736 | bytes 6291456 | tf_op jit(solution)/shard_map/attend_own/pallas_call | solution.py:75
  18.1 6.2 %all-to-all-done = bf16[32,2,16,256]{3,2,1,0:T(8,128)(2,1)S(1)} async-done(((bf16[32,2,16,256]{3,2,1,0:T(8,128)(2,1)}), bf16[32,2,16,256]{3,2,1,0:T(8,128)(2,1)S(1)}, u32[]{:S(2)}, u32[]{:S(2)}) %all-to-all-start) | async-done | bytes 524320 | tf_op jit(solution)/shard_map/all_to_all | solution.py:247
  24.3 0.0 copy-start.3
  24.3 1.6 %gather_fusion = bf16[128,16,256]{2,1,0:T(8,128)(2,1)} fusion(bf16[64,16,256]{2,1,0:T(8,128)(2,1)S(1)} %bitcast.2, s32[1024]{0:T(1024)S(1)} %pad_clamp_fusion), kind=kCustom, calls=%fused_computation | custom fusion | bytes 2097664 | tf_op jit(solution)/shard_map/gather | solution.py:251
  25.9 3.6 %all-to-all-start.1 = ((bf16[32,4,16,256]{3,2,1,0:T(8,128)(2,1)}), bf16[32,4,16,256]{3,2,1,0:T(8,128)(2,1)S(1)}, u32[]{:S(2)}, u32[]{:S(2)}) async-start(bf16[32,4,16,256]{3,2,1,0:T(8,128)(2,1)} %bitcast.3), calls=%async_computation.1 | async-start | bytes 2097152 | tf_op jit(solution)/shard_map/all_to_all | solution.py:252
  29.5 0.2 fusion.usable
  29.8 26.0 %all-to-all-done.1.routed_ref = bf16[32,4,16,256]{3,2,1,0:T(8,128)(2,1)S(1)} async-done(((bf16[32,4,16,256]{3,2,1,0:T(8,128)(2,1)}), bf16[32,4,16,256]{3,2,1,0:T(8,128)(2,1)S(1)}, u32[]{:S(2)}, u32[]{:S(2)}) %all-to-all-start.1) | async-done | bytes 1048608 | tf_op jit(solution)/shard_map/all_to_all | solution.py:252
  55.8 0.0 copy-done.3
  55.8 10.0 %attend_routed.1 = bf16[512,2048]{1,0:T(8,128)(2,1)} custom-call(s32[2,2]{1,0:T(2,128)S(1)} %fusion.usable, bf16[512,2048]{1,0:T(8,128)(2,1)S(1)} %copy-done.3, bf16[512,256]{1,0:T(8,128)(2,1)S(1)} %copy-done.1, f32[2048,512]{1,0:T(8,128)} %get-tuple-element.9.sum_hbm, f32[32,512]{1,0:T(8,128)S(1)} %get-tuple-element.11.stat_ref, ...), custom_call_target="tpu_custom_call" | custom-call | flops 4294967296 | bytes 9437184 | tf_op jit(solution)/shard_map/attend_routed/pallas_call | solution.py:203
  (3 shorter events, 0.0 us)
Async XLA Ops:
  0.0 9.6 %copy-start.1 = (bf16[512,256]{1,0:T(8,128)(2,1)S(1)}, bf16[512,256]{1,0:T(8,128)(2,1)}, u32[]{:S(2)}) copy-start(bf16[512,256]{1,0:T(8,128)(2,1)} %first_key_ref.1) | copy-start | bytes 786436
  0.0 9.6 %copy-start = (bf16[512,256]{1,0:T(8,128)(2,1)S(1)}, bf16[512,256]{1,0:T(8,128)(2,1)}, u32[]{:S(2)}) copy-start(bf16[512,256]{1,0:T(8,128)(2,1)} %v_ref.3) | copy-start | bytes 786436
  0.0 9.3 %copy-start.4 = (s32[32,2,2]{0,2,1:T(2,128)S(1)}, s32[32,2,2]{0,2,1:T(2,128)}, u32[]{:S(2)}) copy-start(s32[32,2,2]{0,2,1:T(2,128)} %param.7) | copy-start | bytes 1540
  2.0 22.3 %all-to-all-start = ((bf16[32,2,16,256]{3,2,1,0:T(8,128)(2,1)}), bf16[32,2,16,256]{3,2,1,0:T(8,128)(2,1)S(1)}, u32[]{:S(2)}, u32[]{:S(2)}) async-start(bf16[32,2,16,256]{3,2,1,0:T(8,128)(2,1)} %pack.1), calls=%async_computation | async-start | bytes 1048576 | tf_op jit(solution)/shard_map/all_to_all | solution.py:247
  9.6 1.6 %copy-start.2 = (bf16[512,2048]{1,0:T(8,128)(2,1)S(1)}, bf16[512,2048]{1,0:T(8,128)(2,1)}, u32[]{:S(2)}) copy-start(bf16[512,2048]{1,0:T(8,128)(2,1)} %q_ref.3) | copy-start | bytes 6291460
  24.3 31.5 %copy-start.3 = (bf16[512,2048]{1,0:T(8,128)(2,1)S(1)}, bf16[512,2048]{1,0:T(8,128)(2,1)}, u32[]{:S(2)}) copy-start(bf16[512,2048]{1,0:T(8,128)(2,1)} %q_ref.3) | copy-start | bytes 6291460
  25.9 29.9 %all-to-all-start.1 = ((bf16[32,4,16,256]{3,2,1,0:T(8,128)(2,1)}), bf16[32,4,16,256]{3,2,1,0:T(8,128)(2,1)S(1)}, u32[]{:S(2)}, u32[]{:S(2)}) async-start(bf16[32,4,16,256]{3,2,1,0:T(8,128)(2,1)} %bitcast.3), calls=%async_computation.1 | async-start | bytes 2097152 | tf_op jit(solution)/shard_map/all_to_all | solution.py:252

commit v5 on v4

--- a/solution.py
+++ b/solution.py
@@ -15,7 +15,7 @@
 TILE = 256
 CHUNK = 256
 EARLY = 4
-CUT = 12
+CUT = 10
 STEP = GROUP
 ROOM = 2.0**100
 EXPONENT = HD ** (-0.5) * math.log2(math.e)
@@ -242,14 +242,21 @@
     count = lax.axis_size(AXES)
     me = lax.axis_index(AXES)
     kv_heads = keys.shape[1] // HD
+    turn = count // 2
+    order = [(p + turn) % count for p in range(count)]
     usable = (lax.dynamic_index_in_dim(chosen, me, 0, keepdims=False) < me).astype(jnp.int32)
-    wanted = chosen * kv_heads + jnp.arange(kv_heads, dtype=jnp.int32)[None, :, None]
-    table = lax.all_to_all(pack(keys, values, count), AXES, 0, 0, tiled=True)
+    place = (jnp.roll(chosen, -turn, axis=0) + (count - turn)) % count
+    wanted = place * kv_heads + jnp.arange(kv_heads, dtype=jnp.int32)[None, :, None]
+
+    def exchange(rows):
+        return lax.all_to_all(rows, AXES, 0, 0, axis_index_groups=[order], tiled=True)
+
+    table = exchange(pack(keys, values, count))
     table = table.reshape(count * kv_heads, BS // count, 2 * HD)
     own_sum, own_stat = attend_own(queries, keys, values)
     wanted, own_stat = lax.optimization_barrier((wanted.reshape(-1), own_stat))
     request = table[wanted].reshape(count, kv_heads * 2, BS // count, 2 * HD)
-    routed = lax.all_to_all(request, AXES, 0, 0, tiled=True)
+    routed = exchange(request)
     return attend_routed(usable, queries, keys, own_sum, own_stat, routed)
 
 

time: 66.3 us -> 66.1 us (level)
  no operation moved by 1% of the time
where the time goes in v5:
time: 66.1 us; the launch traced here: 65.7 us
  waiting for transfers between devices  31.9 us (48%)
  Pallas kernels  18.7 us (28%)
  starting transfers between devices  10.9 us (16%)
  local copies, waits for them, and re-layouts  3.7 us (6%)
    all_to_all x2, waiting for transfers between devices, exchange(): lax.all_to_all(rows, AXES, 0, 0, axis_index_groups=[order], tiled=True)  31.9 us
    all_to_all x2, starting transfers between devices, exchange(): lax.all_to_all(rows, AXES, 0, 0, axis_index_groups=[order], tiled=True)  10.9 us
    pallas_call x1, Pallas kernels, attend_routed(): pl.pallas_call(routed_kernel, in_specs=[pl.BlockSpec(memory_space=pltpu.S...  9.79 us
    pallas_call x1, Pallas kernels, attend_own(): pl.pallas_call(own_kernel, grid=(heads // STEP,), in_specs=[pl.BlockSpec(...  6.93 us
    pallas_call x1, Pallas kernels, pack(): pl.pallas_call(pack_kernel, out_shape=jax.ShapeDtypeStruct(shape, keys.dt...  1.98 us
    gather x1, local copies, waits for them, and re-layouts, resident(): request = table[wanted].reshape(count, kv_heads * 2, BS // count, 2 * HD)  1.61 us
    unnamed x10, local copies, waits for them, and re-layouts  1.6 us
  transfers between devices with their start and end apart: 2, of which 2 were waited for; matrix products, arithmetic and copies ran while one was open for 1% of the time, Pallas kernels for 11%

profile of v5, /device:TPU:0, one launch (start us, length us, event | category | flops | bytes accessed | tf_op | source)
XLA Modules:
  0.0 65.7 jit_solution(4153483232761331316)
XLA Ops:
  0.0 0.0 copy-start.1
  0.0 0.0 copy-start
  0.0 0.0 copy-start.4
  0.0 2.0 %pack.1 = bf16[32,2,16,256]{3,2,1,0:T(8,128)(2,1)} custom-call(bf16[512,256]{1,0:T(8,128)(2,1)} %first_key_ref.1, bf16[512,256]{1,0:T(8,128)(2,1)} %v_ref.3), custom_call_target="tpu_custom_call" | custom-call | tf_op jit(solution)/shard_map/pack/pallas_call | solution.py:236
  2.0 7.3 %all-to-all-start = ((bf16[32,2,16,256]{3,2,1,0:T(8,128)(2,1)}), bf16[32,2,16,256]{3,2,1,0:T(8,128)(2,1)S(1)}, u32[]{:S(2)}, u32[]{:S(2)}) async-start(bf16[32,2,16,256]{3,2,1,0:T(8,128)(2,1)} %pack.1), calls=%async_computation | async-start | bytes 1048576 | tf_op jit(solution)/shard_map/all_to_all | solution.py:252
  9.3 0.0 copy-done.4
  9.3 0.1 fusion.4
  9.4 0.1 add_add_fusion
  9.5 0.1 copy.6
  9.6 0.2 add.45
  9.7 0.1 add.48
  9.9 0.0 copy-done.1
  9.9 0.0 copy-done
  9.9 0.0 copy-start.2
  9.9 1.6 %copy-done.2 = bf16[512,2048]{1,0:T(8,128)(2,1)S(1)} copy-done((bf16[512,2048]{1,0:T(8,128)(2,1)S(1)}, bf16[512,2048]{1,0:T(8,128)(2,1)}, u32[]{:S(2)}) %copy-start.2) | copy-done | bytes 2097176
  11.5 6.9 %attend_own.1 = (f32[2048,512]{1,0:T(8,128)}, f32[32,512]{1,0:T(8,128)S(1)}) custom-call(bf16[512,2048]{1,0:T(8,128)(2,1)S(1)} %copy-done.2, bf16[512,256]{1,0:T(8,128)(2,1)S(1)} %copy-done.1, bf16[512,256]{1,0:T(8,128)(2,1)S(1)} %copy-done), custom_call_target="tpu_custom_call" | custom-call | flops 1610612736 | bytes 6291456 | tf_op jit(solution)/shard_map/attend_own/pallas_call | solution.py:75
  18.5 5.8 %all-to-all-done = bf16[32,2,16,256]{3,2,1,0:T(8,128)(2,1)S(1)} async-done(((bf16[32,2,16,256]{3,2,1,0:T(8,128)(2,1)}), bf16[32,2,16,256]{3,2,1,0:T(8,128)(2,1)S(1)}, u32[]{:S(2)}, u32[]{:S(2)}) %all-to-all-start) | async-done | bytes 524320 | tf_op jit(solution)/shard_map/all_to_all | solution.py:252
  24.3 0.0 copy-start.3
  24.3 1.6 %gather_fusion = bf16[128,16,256]{2,1,0:T(8,128)(2,1)} fusion(bf16[64,16,256]{2,1,0:T(8,128)(2,1)S(1)} %bitcast.2, s32[1024]{0:T(1024)S(1)} %pad_clamp_fusion), kind=kCustom, calls=%fused_computation | custom fusion | bytes 2097664 | tf_op jit(solution)/shard_map/gather | solution.py:258
  25.9 3.6 %all-to-all-start.1 = ((bf16[32,4,16,256]{3,2,1,0:T(8,128)(2,1)}), bf16[32,4,16,256]{3,2,1,0:T(8,128)(2,1)S(1)}, u32[]{:S(2)}, u32[]{:S(2)}) async-start(bf16[32,4,16,256]{3,2,1,0:T(8,128)(2,1)} %bitcast.3), calls=%async_computation.1 | async-start | bytes 2097152 | tf_op jit(solution)/shard_map/all_to_all | solution.py:252
  29.5 0.2 fusion.usable
  29.8 26.0 %all-to-all-done.1.routed_ref = bf16[32,4,16,256]{3,2,1,0:T(8,128)(2,1)S(1)} async-done(((bf16[32,4,16,256]{3,2,1,0:T(8,128)(2,1)}), bf16[32,4,16,256]{3,2,1,0:T(8,128)(2,1)S(1)}, u32[]{:S(2)}, u32[]{:S(2)}) %all-to-all-start.1) | async-done | bytes 1048608 | tf_op jit(solution)/shard_map/all_to_all | solution.py:252
  55.8 0.0 copy-done.3
  55.8 9.8 %attend_routed.1 = bf16[512,2048]{1,0:T(8,128)(2,1)} custom-call(s32[2,2]{1,0:T(2,128)S(1)} %fusion.usable, bf16[512,2048]{1,0:T(8,128)(2,1)S(1)} %copy-done.3, bf16[512,256]{1,0:T(8,128)(2,1)S(1)} %copy-done.1, f32[2048,512]{1,0:T(8,128)} %get-tuple-element.9.sum_hbm, f32[32,512]{1,0:T(8,128)S(1)} %get-tuple-element.11.stat_ref, ...), custom_call_target="tpu_custom_call" | custom-call | flops 4294967296 | bytes 9437184 | tf_op jit(solution)/shard_map/attend_routed/pallas_call | solution.py:203
  (4 shorter events, 0.0 us)
Async XLA Ops:
  0.0 9.9 %copy-start.1 = (bf16[512,256]{1,0:T(8,128)(2,1)S(1)}, bf16[512,256]{1,0:T(8,128)(2,1)}, u32[]{:S(2)}) copy-start(bf16[512,256]{1,0:T(8,128)(2,1)} %first_key_ref.1) | copy-start | bytes 786436
  0.0 9.9 %copy-start = (bf16[512,256]{1,0:T(8,128)(2,1)S(1)}, bf16[512,256]{1,0:T(8,128)(2,1)}, u32[]{:S(2)}) copy-start(bf16[512,256]{1,0:T(8,128)(2,1)} %v_ref.3) | copy-start | bytes 786436
  0.0 9.3 %copy-start.4 = (s32[32,2,2]{0,2,1:T(2,128)S(1)}, s32[32,2,2]{0,2,1:T(2,128)}, u32[]{:S(2)}) copy-start(s32[32,2,2]{0,2,1:T(2,128)} %param.7) | copy-start | bytes 1540
  2.0 22.3 %all-to-all-start = ((bf16[32,2,16,256]{3,2,1,0:T(8,128)(2,1)}), bf16[32,2,16,256]{3,2,1,0:T(8,128)(2,1)S(1)}, u32[]{:S(2)}, u32[]{:S(2)}) async-start(bf16[32,2,16,256]{3,2,1,0:T(8,128)(2,1)} %pack.1), calls=%async_computation | async-start | bytes 1048576 | tf_op jit(solution)/shard_map/all_to_all | solution.py:252
  9.9 1.6 %copy-start.2 = (bf16[512,2048]{1,0:T(8,128)(2,1)S(1)}, bf16[512,2048]{1,0:T(8,128)(2,1)}, u32[]{:S(2)}) copy-start(bf16[512,2048]{1,0:T(8,128)(2,1)} %q_ref.3) | copy-start | bytes 6291460
  24.3 31.5 %copy-start.3 = (bf16[512,2048]{1,0:T(8,128)(2,1)S(1)}, bf16[512,2048]{1,0:T(8,128)(2,1)}, u32[]{:S(2)}) copy-start(bf16[512,2048]{1,0:T(8,128)(2,1)} %q_ref.3) | copy-start | bytes 6291460
  25.9 29.9 %all-to-all-start.1 = ((bf16[32,4,16,256]{3,2,1,0:T(8,128)(2,1)}), bf16[32,4,16,256]{3,2,1,0:T(8,128)(2,1)S(1)}, u32[]{:S(2)}, u32[]{:S(2)}) async-start(bf16[32,4,16,256]{3,2,1,0:T(8,128)(2,1)} %bitcast.3), calls=%async_computation.1 | async-start | bytes 2097152 | tf_op jit(solution)/shard_map/all_to_all | solution.py:252

commit v6 on v4

--- a/solution.py
+++ b/solution.py
@@ -167,11 +167,12 @@
 
     staggered([(h, t) for h in range(heads) for t in range(0, BS, TILE)], first, second)
     take_out(1, CUT, heads - CUT).start()
+    in_range = functools.reduce(jnp.logical_and, [total < ROOM for total in seen])
+    redo = jnp.logical_not(jnp.all(in_range))
     take_out(0, 0, CUT).wait()
     take_out(1, CUT, heads - CUT).wait()
-    in_range = functools.reduce(jnp.logical_and, [total < ROOM for total in seen])
-
-    @pl.when(jnp.logical_not(jnp.all(in_range)))
+
+    @pl.when(redo)
     def _():
         for g in range(kv_heads):
             all_keys = jnp.concatenate([keys[g, s] for s in range(2)], axis=0)

time: 66.3 us -> 65.9 us (level)
  no operation moved by 1% of the time
where the time goes in v6:
time: 65.9 us; the launch traced here: 65.5 us
  waiting for transfers between devices  32.2 us (49%)
  Pallas kernels  18.5 us (28%)
  starting transfers between devices  10.9 us (17%)
  local copies, waits for them, and re-layouts  3.46 us (5%)
    all_to_all x1, waiting for transfers between devices, resident(): routed = lax.all_to_all(request, AXES, 0, 0, tiled=True)  26 us
    pallas_call x1, Pallas kernels, attend_routed(): pl.pallas_call(routed_kernel, in_specs=[pl.BlockSpec(memory_space=pltpu.S...  9.6 us
    all_to_all x1, starting transfers between devices, resident(): table = lax.all_to_all(pack(keys, values, count), AXES, 0, 0, tiled=True)  7.3 us
    pallas_call x1, Pallas kernels, attend_own(): pl.pallas_call(own_kernel, grid=(heads // STEP,), in_specs=[pl.BlockSpec(...  6.93 us
    all_to_all x1, waiting for transfers between devices, resident(): table = lax.all_to_all(pack(keys, values, count), AXES, 0, 0, tiled=True)  6.17 us
    all_to_all x1, starting transfers between devices, resident(): routed = lax.all_to_all(request, AXES, 0, 0, tiled=True)  3.62 us
    pallas_call x1, Pallas kernels, pack(): pl.pallas_call(pack_kernel, out_shape=jax.ShapeDtypeStruct(shape, keys.dt...  1.98 us
    gather x1, local copies, waits for them, and re-layouts, resident(): request = table[wanted].reshape(count, kv_heads * 2, BS // count, 2 * HD)  1.61 us
  transfers between devices with their start and end apart: 2, of which 2 were waited for; matrix products, arithmetic and copies ran while one was open for 1% of the time, Pallas kernels for 11%

profile of v6, /device:TPU:0, one launch (start us, length us, event | category | flops | bytes accessed | tf_op | source)
XLA Modules:
  0.0 65.5 jit_solution(13184285140691670135)
XLA Ops:
  0.0 0.0 copy-start.1
  0.0 0.0 copy-start
  0.0 0.0 copy-start.4
  0.0 2.0 %pack.1 = bf16[32,2,16,256]{3,2,1,0:T(8,128)(2,1)} custom-call(bf16[512,256]{1,0:T(8,128)(2,1)} %first_key_ref.1, bf16[512,256]{1,0:T(8,128)(2,1)} %v_ref.3), custom_call_target="tpu_custom_call" | custom-call | tf_op jit(solution)/shard_map/pack/pallas_call | solution.py:237
  2.0 7.3 %all-to-all-start = ((bf16[32,2,16,256]{3,2,1,0:T(8,128)(2,1)}), bf16[32,2,16,256]{3,2,1,0:T(8,128)(2,1)S(1)}, u32[]{:S(2)}, u32[]{:S(2)}) async-start(bf16[32,2,16,256]{3,2,1,0:T(8,128)(2,1)} %pack.1), calls=%async_computation | async-start | bytes 1048576 | tf_op jit(solution)/shard_map/all_to_all | solution.py:248
  9.3 0.0 copy-done.4
  9.3 0.1 copy.6
  9.4 0.1 reshape.13
  9.6 0.0 copy-done.1
  9.6 0.0 copy-done
  9.6 0.0 copy-start.2
  9.6 1.6 %copy-done.2 = bf16[512,2048]{1,0:T(8,128)(2,1)S(1)} copy-done((bf16[512,2048]{1,0:T(8,128)(2,1)S(1)}, bf16[512,2048]{1,0:T(8,128)(2,1)}, u32[]{:S(2)}) %copy-start.2) | copy-done | bytes 2097176
  11.2 6.9 %attend_own.1 = (f32[2048,512]{1,0:T(8,128)}, f32[32,512]{1,0:T(8,128)S(1)}) custom-call(bf16[512,2048]{1,0:T(8,128)(2,1)S(1)} %copy-done.2, bf16[512,256]{1,0:T(8,128)(2,1)S(1)} %copy-done.1, bf16[512,256]{1,0:T(8,128)(2,1)S(1)} %copy-done), custom_call_target="tpu_custom_call" | custom-call | flops 1610612736 | bytes 6291456 | tf_op jit(solution)/shard_map/attend_own/pallas_call | solution.py:75
  18.1 6.2 %all-to-all-done = bf16[32,2,16,256]{3,2,1,0:T(8,128)(2,1)S(1)} async-done(((bf16[32,2,16,256]{3,2,1,0:T(8,128)(2,1)}), bf16[32,2,16,256]{3,2,1,0:T(8,128)(2,1)S(1)}, u32[]{:S(2)}, u32[]{:S(2)}) %all-to-all-start) | async-done | bytes 524320 | tf_op jit(solution)/shard_map/all_to_all | solution.py:248
  24.3 0.0 copy-start.3
  24.3 1.6 %gather_fusion = bf16[128,16,256]{2,1,0:T(8,128)(2,1)} fusion(bf16[64,16,256]{2,1,0:T(8,128)(2,1)S(1)} %bitcast.2, s32[1024]{0:T(1024)S(1)} %pad_clamp_fusion), kind=kCustom, calls=%fused_computation | custom fusion | bytes 2097664 | tf_op jit(solution)/shard_map/gather | solution.py:252
  25.9 3.6 %all-to-all-start.1 = ((bf16[32,4,16,256]{3,2,1,0:T(8,128)(2,1)}), bf16[32,4,16,256]{3,2,1,0:T(8,128)(2,1)S(1)}, u32[]{:S(2)}, u32[]{:S(2)}) async-start(bf16[32,4,16,256]{3,2,1,0:T(8,128)(2,1)} %bitcast.3), calls=%async_computation.1 | async-start | bytes 2097152 | tf_op jit(solution)/shard_map/all_to_all | solution.py:253
  29.5 0.2 fusion.usable
  29.8 26.0 %all-to-all-done.1.routed_ref = bf16[32,4,16,256]{3,2,1,0:T(8,128)(2,1)S(1)} async-done(((bf16[32,4,16,256]{3,2,1,0:T(8,128)(2,1)}), bf16[32,4,16,256]{3,2,1,0:T(8,128)(2,1)S(1)}, u32[]{:S(2)}, u32[]{:S(2)}) %all-to-all-start.1) | async-done | bytes 1048608 | tf_op jit(solution)/shard_map/all_to_all | solution.py:253
  55.8 0.0 copy-done.3
  55.8 9.6 %attend_routed.1 = bf16[512,2048]{1,0:T(8,128)(2,1)} custom-call(s32[2,2]{1,0:T(2,128)S(1)} %fusion.usable, bf16[512,2048]{1,0:T(8,128)(2,1)S(1)} %copy-done.3, bf16[512,256]{1,0:T(8,128)(2,1)S(1)} %copy-done.1, f32[2048,512]{1,0:T(8,128)} %get-tuple-element.9.sum_hbm, f32[32,512]{1,0:T(8,128)S(1)} %get-tuple-element.11.stat_ref, ...), custom_call_target="tpu_custom_call" | custom-call | flops 4294967296 | bytes 9437184 | tf_op jit(solution)/shard_map/attend_routed/pallas_call | solution.py:204
  (3 shorter events, 0.0 us)
Async XLA Ops:
  0.0 9.6 %copy-start.1 = (bf16[512,256]{1,0:T(8,128)(2,1)S(1)}, bf16[512,256]{1,0:T(8,128)(2,1)}, u32[]{:S(2)}) copy-start(bf16[512,256]{1,0:T(8,128)(2,1)} %first_key_ref.1) | copy-start | bytes 786436
  0.0 9.6 %copy-start = (bf16[512,256]{1,0:T(8,128)(2,1)S(1)}, bf16[512,256]{1,0:T(8,128)(2,1)}, u32[]{:S(2)}) copy-start(bf16[512,256]{1,0:T(8,128)(2,1)} %v_ref.3) | copy-start | bytes 786436
  0.0 9.3 %copy-start.4 = (s32[32,2,2]{0,2,1:T(2,128)S(1)}, s32[32,2,2]{0,2,1:T(2,128)}, u32[]{:S(2)}) copy-start(s32[32,2,2]{0,2,1:T(2,128)} %param.7) | copy-start | bytes 1540
  2.0 22.3 %all-to-all-start = ((bf16[32,2,16,256]{3,2,1,0:T(8,128)(2,1)}), bf16[32,2,16,256]{3,2,1,0:T(8,128)(2,1)S(1)}, u32[]{:S(2)}, u32[]{:S(2)}) async-start(bf16[32,2,16,256]{3,2,1,0:T(8,128)(2,1)} %pack.1), calls=%async_computation | async-start | bytes 1048576 | tf_op jit(solution)/shard_map/all_to_all | solution.py:248
  9.6 1.6 %copy-start.2 = (bf16[512,2048]{1,0:T(8,128)(2,1)S(1)}, bf16[512,2048]{1,0:T(8,128)(2,1)}, u32[]{:S(2)}) copy-start(bf16[512,2048]{1,0:T(8,128)(2,1)} %q_ref.3) | copy-start | bytes 6291460
  24.3 31.5 %copy-start.3 = (bf16[512,2048]{1,0:T(8,128)(2,1)S(1)}, bf16[512,2048]{1,0:T(8,128)(2,1)}, u32[]{:S(2)}) copy-start(bf16[512,2048]{1,0:T(8,128)(2,1)} %q_ref.3) | copy-start | bytes 6291460
  25.9 29.9 %all-to-all-start.1 = ((bf16[32,4,16,256]{3,2,1,0:T(8,128)(2,1)}), bf16[32,4,16,256]{3,2,1,0:T(8,128)(2,1)S(1)}, u32[]{:S(2)}, u32[]{:S(2)}) async-start(bf16[32,4,16,256]{3,2,1,0:T(8,128)(2,1)} %bitcast.3), calls=%async_computation.1 | async-start | bytes 2097152 | tf_op jit(solution)/shard_map/all_to_all | solution.py:253
